TPU v7x, 32 devices: a whole 2x2x4 slice. The times are simulated.
32 devices in a mesh: batch: 8 (over z, x), seq: 4 (over y, core).
Axes of the slice: x: 2, y: 2, z: 4, core: 2. Of those that a mesh axis runs over, the one named last changes fastest.
Arguments:
- tokens: bfloat16 [8, 6144, 512], P('batch', 'seq'), may hold values from -6 to 6
- qkv_weight: bfloat16 [3, 512, 512], P(None, 'batch', 'seq'), may hold values from -0.25 to 0.25
- out_proj: bfloat16 [512, 512], P('batch', 'seq'), may hold values from -6 to 6
- in_weight: bfloat16 [512, 2048], P('batch', 'seq'), may hold values from -0.25 to 0.25
- out_weight: bfloat16 [2048, 512], P('seq', 'batch'), may hold values from -0.125 to 0.125
- norm_params: bfloat16 [4, 512], P('seq', 'batch')
- rand_features: bfloat16 [8, 64, 256], replicated, may hold values from -6 to 6
- long_start: int32 [8], P('batch'), may hold values from 256 to 768
- masked_pos: int32 [8, 1536], P('batch', 'seq'), may hold values from 0 to 1535, as said below
- masked_count: int32 [8, 4], P('batch', 'seq'), may hold values from 76 to 384, as said below
- masked_grad: bfloat16 [8, 1536, 512], P('batch', 'seq'), may hold values from -6 to 6
Outputs:
- mixed: bfloat16 [8, 6144, 512], P('batch', 'seq')
- tokens_grad: float32 [8, 6144, 512], P('batch', 'seq')
- qkv_grad: float32 [3, 512, 512], P(None, 'batch', 'seq')
- out_proj_grad: float32 [512, 512], P('batch', 'seq')
- in_grad: float32 [512, 2048], P('batch', 'seq')
- out_grad: float32 [2048, 512], P('seq', 'batch')
- norm_grad: float32 [4, 512], P('seq', 'batch')
Inputs may be any that keep to these rules, and one draw needn't show every extreme that they name: `masked_pos`: within each block of 384 slots the positions are distinct. `masked_count`: some block is full in every draw. `long_start`: each group holds one sequence of 5120 tokens starting here, one sequence before it and one after it.
All inputs are finite; a program needn't handle non-finite values.
Results may differ from a plain program's by a relative error of at most 0.03.
Values may be sent and summed in bfloat16 or wider, within the bound.
A program may use at most 192 MiB of HBM per device.

v0:
```python
import jax
import jax.numpy as jnp
from jax import lax
from jax.sharding import PartitionSpec as P

SHORT = 1024


EPS = 1e-05


def layer_norm_parts(values, gain_row, shift_row):
    row_mean = jnp.mean(values, axis=-1, keepdims=True)
    centred = values - row_mean
    row_var = jnp.mean(centred * centred, axis=-1, keepdims=True)
    inverse = lax.rsqrt(row_var + EPS)
    unit_rows = centred * inverse
    return (unit_rows * gain_row + shift_row, unit_rows, inverse)


def layer_norm_back(incoming, unit_rows, inverse, gain_row):
    scaled = incoming * gain_row
    inner = (
        scaled
        - jnp.mean(scaled, axis=-1, keepdims=True)
        - unit_rows * jnp.mean(scaled * unit_rows, axis=-1, keepdims=True)
    )
    return (inner * inverse, jnp.sum(incoming * unit_rows, axis=0), jnp.sum(incoming, axis=0))


def exact_gelu(values):
    return jax.nn.gelu(values, approximate=False)


def positive_raw(values, feature_dirs):
    feat_scale = values.shape[-1] ** (-0.25)
    projected = feat_scale * jnp.einsum(
        "rhd,hdm->rhm", values, feature_dirs, preferred_element_type=jnp.float32
    )
    values_wide = values.astype(jnp.float32)
    sq_norm = jnp.sum(values_wide * values_wide, axis=-1, keepdims=True)
    return jnp.exp(projected - 0.5 * feat_scale * feat_scale * sq_norm) * feature_dirs.shape[
        -1
    ] ** (-0.5)


def positive_back(feat_grad, raw_feat, values, feature_dirs):
    feat_scale = values.shape[-1] ** (-0.25)
    exponent_grad = feat_grad * raw_feat
    direct = feat_scale * jnp.einsum(
        "rhm,hdm->rhd",
        exponent_grad.astype(jnp.bfloat16),
        feature_dirs,
        preferred_element_type=jnp.float32,
    )
    values_wide = values.astype(jnp.float32)
    norm_part = (
        feat_scale * feat_scale * values_wide * jnp.sum(exponent_grad, axis=-1, keepdims=True)
    )
    return (direct - norm_part).astype(jnp.bfloat16)


def place_two(first_sel, second_sel, first_val, second_val):
    shape_tail = (1,) * first_val.ndim
    return (
        first_sel.reshape((3,) + shape_tail) * first_val[None]
        + second_sel.reshape((3,) + shape_tail) * second_val[None]
    )


def pick_one(stacked, which):
    return lax.dynamic_index_in_dim(stacked, which, 0, keepdims=False)


def on_device(
    tokens,
    qkv_weight,
    out_proj,
    in_weight,
    out_weight,
    norm_params,
    rand_features,
    long_start,
    masked_pos,
    masked_count,
    masked_grad,
):
    low_type = jnp.bfloat16
    wider_number_type = jnp.float32
    part_qkv, part_out, part_in, part_down, part_norm = (
        lax.all_gather(qkv_weight, "seq", axis=2, tiled=True),
        lax.all_gather(out_proj, "seq", axis=1, tiled=True),
        lax.all_gather(in_weight, "seq", axis=1, tiled=True),
        lax.all_gather(out_weight, "seq", axis=0, tiled=True),
        lax.all_gather(norm_params, "seq", axis=0, tiled=True),
    )
    w_qkv, w_out, w_in, w_down, norm_low = (
        lax.all_gather(part_qkv, "batch", axis=1, tiled=True),
        lax.all_gather(part_out, "batch", axis=0, tiled=True),
        lax.all_gather(part_in, "batch", axis=0, tiled=True),
        lax.all_gather(part_down, "batch", axis=1, tiled=True),
        lax.all_gather(part_norm, "batch", axis=1, tiled=True),
    )
    norm_wide = norm_low.astype(wider_number_type)
    row_count = tokens.shape[1]
    model_width = tokens.shape[2]
    head_count = rand_features.shape[0]
    head_size = rand_features.shape[1]
    seq_index = lax.axis_index("seq")
    seq_last = lax.axis_size("seq") - 1
    position = seq_index * row_count + jnp.arange(row_count, dtype=jnp.int32)
    long_from = long_start[0]
    long_span = lax.axis_size("seq") * row_count - SHORT
    segment = (position >= long_from).astype(jnp.int32) + (
        position >= long_from + long_span
    ).astype(jnp.int32)
    seg_lower = jnp.where(seq_index == 0, 0, 1).astype(jnp.int32)
    seg_upper = jnp.where(seq_index == seq_last, 2, 1).astype(jnp.int32)
    member_upper = ((segment == seg_upper) & (seg_upper != seg_lower)).astype(wider_number_type)
    member_lower = 1.0 - member_upper
    sel_lower = (jnp.arange(3, dtype=jnp.int32) == seg_lower).astype(wider_number_type)
    sel_upper = (jnp.arange(3, dtype=jnp.int32) == seg_upper).astype(wider_number_type) * (
        seg_upper != seg_lower
    ).astype(wider_number_type)
    tokens_wide = tokens[0].astype(wider_number_type)
    normed_wide, unit_one, inverse_one = layer_norm_parts(tokens_wide, norm_wide[0], norm_wide[1])
    normed = normed_wide.astype(low_type)
    query = (
        jnp.dot(normed, w_qkv[0], preferred_element_type=wider_number_type)
        .astype(low_type)
        .reshape(row_count, head_count, head_size)
    )
    key_vecs = (
        jnp.dot(normed, w_qkv[1], preferred_element_type=wider_number_type)
        .astype(low_type)
        .reshape(row_count, head_count, head_size)
    )
    value_vectors = (
        jnp.dot(normed, w_qkv[2], preferred_element_type=wider_number_type)
        .astype(low_type)
        .reshape(row_count, head_count, head_size)
    )
    key_raw = positive_raw(key_vecs, rand_features)
    key_feature_map = key_raw.astype(low_type)
    query_feature_map = positive_raw(query, rand_features).astype(low_type)
    key_bottom_rows = key_feature_map * member_lower.astype(low_type)[:, None, None]
    key_top_rows = key_feature_map * member_upper.astype(low_type)[:, None, None]
    summary_lower = jnp.einsum(
        "jkn,jkp->knp", key_bottom_rows, value_vectors, preferred_element_type=wider_number_type
    )
    summary_upper = jnp.einsum(
        "jkn,jkp->knp", key_top_rows, value_vectors, preferred_element_type=wider_number_type
    )
    total_lower = jnp.einsum(
        "thm,t->hm",
        key_feature_map,
        member_lower.astype(low_type),
        preferred_element_type=wider_number_type,
    )
    total_upper = jnp.einsum(
        "thm,t->hm",
        key_feature_map,
        member_upper.astype(low_type),
        preferred_element_type=wider_number_type,
    )
    summary_part = place_two(sel_lower, sel_upper, summary_lower, summary_upper)
    total_part = place_two(sel_lower, sel_upper, total_lower, total_upper)
    state_summary, total = lax.psum((summary_part, total_part), "seq")
    summary_low = state_summary.astype(low_type)
    total_low = total.astype(low_type)
    sum_bottom_half = pick_one(summary_low, seg_lower)
    sum_top_half = pick_one(summary_low, seg_upper)
    tot_lo = pick_one(total_low, seg_lower)
    tot_hi = pick_one(total_low, seg_upper)
    numerator = member_lower[:, None, None] * jnp.einsum(
        "pox,oxa->poa", query_feature_map, sum_bottom_half, preferred_element_type=wider_number_type
    )
    numerator = numerator + member_upper[:, None, None] * jnp.einsum(
        "pox,oxa->poa", query_feature_map, sum_top_half, preferred_element_type=wider_number_type
    )
    denom = member_lower[:, None] * jnp.einsum(
        "thm,hm->th", query_feature_map, tot_lo, preferred_element_type=wider_number_type
    )
    denom = denom + member_upper[:, None] * jnp.einsum(
        "thm,hm->th", query_feature_map, tot_hi, preferred_element_type=wider_number_type
    )
    heads_out = (numerator / denom[:, :, None]).reshape(row_count, model_width).astype(low_type)
    middle = tokens_wide + jnp.dot(heads_out, w_out, preferred_element_type=wider_number_type)
    normed_two = layer_norm_parts(middle, norm_wide[2], norm_wide[3])[0].astype(low_type)
    upper = jnp.dot(normed_two, w_in, preferred_element_type=wider_number_type)
    activated = exact_gelu(upper).astype(low_type)
    result = (middle + jnp.dot(activated, w_down, preferred_element_type=wider_number_type)).astype(
        low_type
    )
    back_qkv, back_out, back_in, back_down = (w_qkv, w_out, w_in, w_down)
    picked = masked_pos[0]
    in_use = (jnp.arange(picked.shape[0], dtype=jnp.int32) < masked_count[0, 0]).astype(
        wider_number_type
    )
    cot_rows = masked_grad[0].astype(wider_number_type) * in_use[:, None]
    cot_low = cot_rows.astype(low_type)
    middle_rows = middle[picked]
    normed_rows_wide, unit_two, inverse_two = layer_norm_parts(
        middle_rows, norm_wide[2], norm_wide[3]
    )
    normed_rows = normed_rows_wide.astype(low_type)
    upper_rows = jnp.dot(normed_rows, back_in, preferred_element_type=wider_number_type)
    act_rows = exact_gelu(upper_rows).astype(low_type)
    act_grad = jnp.dot(cot_low, back_down.T, preferred_element_type=wider_number_type)
    upper_grad = jax.vjp(exact_gelu, upper_rows)[1](act_grad)[0].astype(low_type)
    grad_in = jnp.einsum(
        "rd,rf->df", normed_rows, upper_grad, preferred_element_type=wider_number_type
    )
    grad_down = jnp.einsum("rf,rd->fd", act_rows, cot_low, preferred_element_type=wider_number_type)
    normed_grad_two = jnp.dot(upper_grad, back_in.T, preferred_element_type=wider_number_type)
    middle_ln, gain_two_grad, bias_two_grad = layer_norm_back(
        normed_grad_two, unit_two, inverse_two, norm_wide[2]
    )
    middle_grad = cot_rows + middle_ln
    attn_grad = middle_grad.astype(low_type)
    grad_out = jnp.einsum(
        "rd,re->de", heads_out[picked], attn_grad, preferred_element_type=wider_number_type
    )
    heads_grad = jnp.dot(attn_grad, back_out.T, preferred_element_type=wider_number_type).reshape(
        -1, head_count, head_size
    )
    query_rows = query[picked]
    query_raw_rows = positive_raw(query_rows, rand_features)
    query_feat_rows = query_feature_map[picked]
    lower_rows = member_lower[picked]
    upper_rows_mask = member_upper[picked]
    numer_rows = numerator[picked]
    denom_rows = denom[picked]
    numerator_gradient = (heads_grad / denom_rows[:, :, None]).astype(low_type)
    denom_grad = (-jnp.sum(heads_grad * numer_rows, axis=-1) / (denom_rows * denom_rows)).astype(
        low_type
    )
    lower_rows_low = lower_rows.astype(low_type)
    upper_rows_low = upper_rows_mask.astype(low_type)
    sgrad_lower = jnp.einsum(
        "wpb,wpq->pbq",
        query_feat_rows,
        numerator_gradient * lower_rows_low[:, None, None],
        preferred_element_type=wider_number_type,
    )
    sgrad_upper = jnp.einsum(
        "wpb,wpq->pbq",
        query_feat_rows,
        numerator_gradient * upper_rows_low[:, None, None],
        preferred_element_type=wider_number_type,
    )
    tgrad_lower = jnp.einsum(
        "rhm,rh->hm",
        query_feat_rows,
        denom_grad * lower_rows_low[:, None],
        preferred_element_type=wider_number_type,
    )
    tgrad_upper = jnp.einsum(
        "rhm,rh->hm",
        query_feat_rows,
        denom_grad * upper_rows_low[:, None],
        preferred_element_type=wider_number_type,
    )
    summary_grad_part = place_two(sel_lower, sel_upper, sgrad_lower, sgrad_upper)
    total_grad_part = place_two(sel_lower, sel_upper, tgrad_lower, tgrad_upper)
    summary_grad, total_grad = (
        lax.psum(summary_grad_part.astype(jnp.bfloat16), "seq").astype(jnp.float32),
        lax.psum(total_grad_part.astype(jnp.bfloat16), "seq").astype(jnp.float32),
    )
    summary_grad_low = summary_grad.astype(low_type)
    segment_grad_bottom = pick_one(summary_grad_low, seg_lower)
    segment_grad_top = pick_one(summary_grad_low, seg_upper)
    tg_lo = pick_one(total_grad, seg_lower)
    tg_hi = pick_one(total_grad, seg_upper)
    denom_grad_wide = denom_grad.astype(wider_number_type)
    query_lower = (
        jnp.einsum(
            "sci,cni->scn",
            numerator_gradient,
            sum_bottom_half,
            preferred_element_type=wider_number_type,
        )
        + denom_grad_wide[:, :, None] * tot_lo.astype(wider_number_type)[None]
    )
    query_upper = (
        jnp.einsum(
            "sci,cni->scn",
            numerator_gradient,
            sum_top_half,
            preferred_element_type=wider_number_type,
        )
        + denom_grad_wide[:, :, None] * tot_hi.astype(wider_number_type)[None]
    )
    query_feat_grad = (
        lower_rows[:, None, None] * query_lower + upper_rows_mask[:, None, None] * query_upper
    )
    key_lower_grad = (
        jnp.einsum(
            "zqy,qiy->zqi",
            value_vectors,
            segment_grad_bottom,
            preferred_element_type=wider_number_type,
        )
        + tg_lo[None]
    )
    key_upper_grad = (
        jnp.einsum(
            "zqy,qiy->zqi",
            value_vectors,
            segment_grad_top,
            preferred_element_type=wider_number_type,
        )
        + tg_hi[None]
    )
    key_feat_grad = (
        member_lower[:, None, None] * key_lower_grad + member_upper[:, None, None] * key_upper_grad
    )
    value_grad = member_lower[:, None, None] * jnp.einsum(
        "pox,oxa->poa",
        key_feature_map,
        segment_grad_bottom,
        preferred_element_type=wider_number_type,
    )
    value_grad = value_grad + member_upper[:, None, None] * jnp.einsum(
        "pox,oxa->poa", key_feature_map, segment_grad_top, preferred_element_type=wider_number_type
    )
    query_grad = positive_back(query_feat_grad, query_raw_rows, query_rows, rand_features).reshape(
        -1, model_width
    )
    key_grad = positive_back(key_feat_grad, key_raw, key_vecs, rand_features).reshape(
        row_count, model_width
    )
    value_low = value_grad.astype(low_type).reshape(row_count, model_width)
    grad_query_w = jnp.einsum(
        "rd,re->de", normed[picked], query_grad, preferred_element_type=wider_number_type
    )
    grad_key_w = jnp.einsum("td,te->de", normed, key_grad, preferred_element_type=wider_number_type)
    grad_value_w = jnp.einsum(
        "td,te->de", normed, value_low, preferred_element_type=wider_number_type
    )
    query_back = jnp.dot(query_grad, back_qkv[0].T, preferred_element_type=wider_number_type)
    normed_grad_one = jnp.dot(
        key_grad, back_qkv[1].T, preferred_element_type=wider_number_type
    ) + jnp.dot(value_low, back_qkv[2].T, preferred_element_type=wider_number_type)
    normed_grad_one = normed_grad_one.at[picked].add(query_back)
    token_ln, gain_one_grad, bias_one_grad = layer_norm_back(
        normed_grad_one, unit_one, inverse_one, norm_wide[0]
    )
    tokens_grad = token_ln.at[picked].add(middle_grad)
    grad_qkv = jnp.stack([grad_query_w, grad_key_w, grad_value_w])
    grad_norm = jnp.stack([gain_one_grad, bias_one_grad, gain_two_grad, bias_two_grad])
    first_qkv, first_out, first_in, first_down, first_norm = (
        lax.psum_scatter(grad_qkv, "batch", scatter_dimension=1, tiled=True),
        lax.psum_scatter(grad_out, "batch", scatter_dimension=0, tiled=True),
        lax.psum_scatter(grad_in, "batch", scatter_dimension=0, tiled=True),
        lax.psum_scatter(grad_down, "batch", scatter_dimension=1, tiled=True),
        lax.psum_scatter(grad_norm, "batch", scatter_dimension=1, tiled=True),
    )
    owned = (
        lax.psum_scatter(
            first_qkv.astype(jnp.bfloat16), "seq", scatter_dimension=2, tiled=True
        ).astype(jnp.float32),
        lax.psum_scatter(
            first_out.astype(jnp.bfloat16), "seq", scatter_dimension=1, tiled=True
        ).astype(jnp.float32),
        lax.psum_scatter(
            first_in.astype(jnp.bfloat16), "seq", scatter_dimension=1, tiled=True
        ).astype(jnp.float32),
        lax.psum_scatter(
            first_down.astype(jnp.bfloat16), "seq", scatter_dimension=0, tiled=True
        ).astype(jnp.float32),
        lax.psum_scatter(
            first_norm.astype(jnp.bfloat16), "seq", scatter_dimension=0, tiled=True
        ).astype(jnp.float32),
    )
    return (result[None], tokens_grad[None], owned[0], owned[1], owned[2], owned[3], owned[4])


def solution(mesh):
    placed = (
        P("batch", "seq", None),
        P(None, "batch", "seq"),
        P("batch", "seq"),
        P("batch", "seq"),
        P("seq", "batch"),
        P("seq", "batch"),
        P(),
        P("batch"),
        P("batch", "seq"),
        P("batch", "seq"),
        P("batch", "seq", None),
    )
    return jax.shard_map(
        on_device,
        mesh=mesh,
        in_specs=placed,
        out_specs=(
            P("batch", "seq", None),
            P("batch", "seq", None),
            P(None, "batch", "seq"),
            P("batch", "seq"),
            P("batch", "seq"),
            P("seq", "batch"),
            P("seq", "batch"),
        ),
        check_vma=False,
    )
```

profile of v0, /device:TPU:0, one launch (start us, length us, event | category | flops | bytes accessed | tf_op | source)
XLA Modules:
  0.0 800.8 jit_solution(8855210189709455943)
XLA Ops:
  7.2 8.8 %all_gather.32 = bf16[3,64,512]{2,1,0:T(8,128)(2,1)} all-gather(bf16[3,64,128]{2,1,0:T(8,128)(2,1)} %param.12), channel_id=1, replica_groups=mesh['batch'=8,'seq'=4] {'seq'}, dimensions={2}, use_global_device_ids=true | all-gather | bytes 245760 | tf_op jit(solution)/shard_map/all_gather | solution.py:91
  16.1 7.0 all_gather.36
  23.2 7.7 all_gather.38
  38.8 20.8 %all-gather.1 = bf16[8,64,4]{1,2,0:T(4,128)(2,1)S(1)} all-gather(bf16[1,64,4]{1,2,0:T(4,128)(2,1)S(1)} %bitcast.337), channel_id=1, replica_groups=mesh['batch'=8,'seq'=4] {'batch'}, dimensions={0}, use_global_device_ids=true | all-gather | bytes 4608 | tf_op jit(solution)/shard_map/all_gather | solution.py:102
  71.3 34.6 %all_gather.35 = bf16[512,512]{1,0:T(8,128)(2,1)} all-gather(bf16[64,512]{1,0:T(8,128)(2,1)S(1)} %all_gather.34), channel_id=1, replica_groups=mesh['batch'=8,'seq'=4] {'batch'}, dimensions={0}, use_global_device_ids=true | all-gather | bytes 589824 | tf_op jit(solution)/shard_map/all_gather | solution.py:99
  128.5 33.7 %all-reduce.6 = (bf16[3,8,256,64]{2,3,1,0:T(8,128)(2,1)}, bf16[3,8,256]{2,1,0:T(8,128)(2,1)S(1)}) all-reduce(f32[3,8,256,64]{2,3,1,0:T(8,128)S(1)} %multiply_add_fusion, f32[3,8,256]{2,1,0:T(8,128)S(1)} %multiply_add_fusion.1), channel_id=1, replica_groups=mesh['batch'=8,'seq'=4] {'seq'}, use_global_device_ids=true, to_apply=%region_3.4 | all-reduce | flops 399360 | bytes 2396160 | tf_op jit(solution)/shard_map/psum | solution.py:168
  178.3 6.3 divide_convert_fusion
  189.5 9.1 %copy.182 = bf16[1536,8,256]{2,1,0:T(8,128)(2,1)} copy(bf16[1536,8,256]{0,2,1:T(8,128)(2,1)} %copy-done.3) | data formatting | bytes 12582912 | tf_op jit(solution)/shard_map/convert_element_type | solution.py:145
  246.4 10.6 %fusion.61 = (f32[384,2048]{1,0:T(8,128)}, f32[384,2048]{1,0:T(8,128)}) fusion(bf16[512,2048]{1,0:T(8,128)(2,1)} %all-gather.8.cloned.1.call-done, f32[384,512]{1,0:T(8,128)} %gather_fusion.1, f32[512]{0:T(512)S(1)} %bitcast.322, f32[512]{0:T(512)S(1)} %bitcast.317, f32[384]{0:T(512)S(1)} %add_rsqrt_fusion.2, f32[384]{0:T(512)S(1)} %broadcast_multiply_fusion.11), kind=kOutput, calls=%fused_computation.85 | convolution fusion | flops 855048192 | bytes 9182208 | tf_op jit(solution)/shard_map/dot_general | solution.py:207
  291.1 10.9 %psum.31 = bf16[3,8,256]{2,1,0:T(8,128)(2,1)S(1)} all-reduce(bf16[3,8,256]{2,1,0:T(8,128)(2,1)S(1)} %add_convert_fusion.8), channel_id=1, replica_groups=mesh['batch'=8,'seq'=4] {'seq'}, use_global_device_ids=true, to_apply=%region_14.15 | all-reduce | flops 6144 | bytes 24576 | tf_op jit(solution)/shard_map/psum | solution.py:268
  311.5 7.4 fusion.124
  318.9 13.2 %fusion.211 = (f32[1536,8]{0,1:T(8,128)S(1)}, bf16[1536,8,256]{0,2,1:T(8,128)(2,1)}) fusion(f32[1536,8]{0,1:T(8,128)S(1)} %broadcast_multiply_fusion.2, f32[8,1536,256]{1,2,0:T(8,128)} %get-tuple-element.78, f32[8,256]{1,0:T(8,128)S(1)} %copy-done.45, bf16[1536,8,64]{0,2,1:T(8,128)(2,1)S(1)} %bitcast.308, bf16[3,8,256,64]{2,3,1,0:T(8,128)(2,1)S(1)} %copy-done.26, ...), kind=kOutput, calls=%fused_computation.298 | convolution fusion | flops 437243904 | bytes 33423364 | tf_op jit(solution)/shard_map/zqy,qiy->zqi/dot_general | solution.py:307
  343.7 7.0 scatter_fusion
  395.1 61.0 %reduce-scatter.16.cloned.1.call-done = f32[3,64,512]{2,1,0:T(8,128)} async-done(((f32[3,512,512]{2,1,0:T(8,128)}), f32[3,64,512]{2,1,0:T(8,128)}) %reduce-scatter.16.cloned.1.call-update) | async-done | bytes 393232 | tf_op jit(solution)/shard_map/reduce_scatter | solution.py:353
  458.6 33.6 %fusion.274 = bf16[1536,2048]{1,0:T(8,128)(2,1)} fusion(bf16[512,2048]{1,0:T(8,128)(2,1)} %all-gather.8.cloned.1.call-done, f32[1536,512]{0,1:T(8,128)} %get-tuple-element.82, f32[512]{0:T(512)S(1)} %bitcast.324, f32[512]{0:T(512)S(1)} %bitcast.321, f32[1536]{0:T(1024)S(1)} %add_rsqrt_fusion, ...), kind=kOutput, calls=%fused_computation.14.clone.clone.clone.clone.clone.clone.clone.clone.1 | convolution fusion | flops 3429629952 | bytes 11550720 | tf_op jit(solution)/shard_map/dot_general | solution.py:190
  492.2 55.1 %reduce-scatter.24.cloned.1.call-done = f32[2048,64]{0,1:T(8,128)} async-done(((f32[2048,512]{0,1:T(8,128)}), f32[2048,64]{0,1:T(8,128)}) %reduce-scatter.24.cloned.1.call-update) | async-done | bytes 524304 | tf_op jit(solution)/shard_map/reduce_scatter | solution.py:356
  549.4 7.8 fusion.82
  558.7 79.9 %reduce-scatter.20.cloned.1.call-done = f32[64,2048]{1,0:T(8,128)} async-done(((f32[512,2048]{1,0:T(8,128)}), f32[64,2048]{1,0:T(8,128)}) %reduce-scatter.20.cloned.1.call-update) | async-done | bytes 524304 | tf_op jit(solution)/shard_map/reduce_scatter | solution.py:355
  648.4 6.4 scatter_fusion.1
  654.8 48.5 %reduce-scatter.32.cloned.1.call-done = f32[64,4]{1,0:T(8,128)} async-done(((f32[512,4]{1,0:T(8,128)}), f32[64,4]{1,0:T(8,128)}) %reduce-scatter.32.cloned.1.call-update) | async-done | bytes 1040
  711.0 14.0 %reduce-scatter.30.cloned.1.call-done = bf16[128,64]{1,0:T(8,128)(2,1)} async-done(((bf16[512,64]{1,0:T(8,128)(2,1)}), bf16[128,64]{1,0:T(8,128)(2,1)}) %reduce-scatter.30.cloned.1.call-update) | async-done | bytes 16400
  726.4 21.0 %reduce-scatter.28.cloned.1.call-done = bf16[128,192]{1,0:T(8,128)(2,1)} async-done(((bf16[512,192]{1,0:T(8,128)(2,1)}), bf16[128,192]{1,0:T(8,128)(2,1)}) %reduce-scatter.28.cloned.1.call-update) | async-done | bytes 49168
  749.2 20.8 %reduce-scatter.26.cloned.1.call-done = bf16[512,64]{0,1:T(8,128)(2,1)} async-done(((bf16[2048,64]{0,1:T(8,128)(2,1)}), bf16[512,64]{0,1:T(8,128)(2,1)}) %reduce-scatter.26.cloned.1.call-update) | async-done | bytes 65552 | tf_op jit(solution)/shard_map/reduce_scatter | solution.py:369
  771.5 21.1 %reduce-scatter.22.cloned.1.call-done = bf16[64,512]{1,0:T(8,128)(2,1)} async-done(((bf16[64,2048]{1,0:T(8,128)(2,1)}), bf16[64,512]{1,0:T(8,128)(2,1)}) %reduce-scatter.22.cloned.1.call-update) | async-done | bytes 65552 | tf_op jit(solution)/shard_map/reduce_scatter | solution.py:366
  (283 shorter events, 238.2 us)
Async XLA Ops:
  7.2 103.4 %copy-start = (bf16[8,64,256]{2,1,0:T(8,128)(2,1)S(1)}, bf16[8,64,256]{2,1,0:T(8,128)(2,1)}, u32[]{:S(2)}) copy-start(bf16[8,64,256]{2,1,0:T(8,128)(2,1)} %param.17) | copy-start | bytes 786436
  7.2 58.8 %copy-start.35 = (bf16[64,128]{1,0:T(8,128)(2,1)S(1)}, bf16[64,128]{1,0:T(8,128)(2,1)}, u32[]{:S(2)}) copy-start(bf16[64,128]{1,0:T(8,128)(2,1)} %param.13) | copy-start | bytes 49156
  7.2 100.8 %all-gather.6.cloned.1.call-start = ((), (), s32[]{:S(2)}) async-start(), calls=%async_computation.9 | async-start | bytes 1769472 | tf_op jit(solution)/shard_map/all_gather | solution.py:98
  16.0 89.9 %copy-start.19 = (bf16[1,1536,512]{2,1,0:T(8,128)(2,1)S(1)}, bf16[1,1536,512]{2,1,0:T(8,128)(2,1)}, u32[]{:S(2)}) copy-start(bf16[1,1536,512]{2,1,0:T(8,128)(2,1)} %param.11) | copy-start | bytes 4718596
  16.0 230.3 %all-gather.8.cloned.1.call-start = ((), (), s32[]{:S(2)}) async-start(), calls=%async_computation.10 | async-start | bytes 2359296 | tf_op jit(solution)/shard_map/all_gather | solution.py:100
  23.1 233.9 %all-gather.10.cloned.1.call-start = ((), (), s32[]{:S(2)}) async-start(), calls=%async_computation.11 | async-start | bytes 2359296 | tf_op jit(solution)/shard_map/all_gather | solution.py:101
  30.9 280.6 %all-reduce.5.cloned.1.call-start = ((), (), s32[]{:S(2)}) async-start(), calls=%async_computation.12 | async-start | bytes 1572864 | tf_op jit(solution)/shard_map/psum | solution.py:267
  30.9 97.3 %copy-start.38 = (f32[3]{0:T(128)}, f32[3]{0:T(128)S(1)}, u32[]{:S(2)}) copy-start(f32[3]{0:T(128)S(1)} %compare_convert_fusion) | copy-start | bytes 40
  32.3 96.0 %copy-start.41 = (f32[3]{0:T(128)}, f32[3]{0:T(128)S(1)}, u32[]{:S(2)}) copy-start(f32[3]{0:T(128)S(1)} %compare_select_fusion.1) | copy-start | bytes 40
  33.6 31.7 %copy-start.29 = (s32[384]{0:T(512)}, s32[384]{0:T(512)S(1)}, u32[]{:S(2)}) copy-start(s32[384]{0:T(512)S(1)} %fusion.174) | copy-start | bytes 4612
  65.3 42.0 %copy-start.47 = (f32[384]{0:T(512)}, f32[384]{0:T(512)S(1)}, u32[]{:S(2)}) copy-start(f32[384]{0:T(512)S(1)} %gather_fusion.3) | copy-start | bytes 4612
  66.0 41.3 %copy-start.31 = (f32[1,512]{1,0:T(1,128)}, f32[1,512]{1,0:T(1,128)S(1)}, u32[]{:S(2)}) copy-start(f32[1,512]{1,0:T(1,128)S(1)} %get-tuple-element.69) | copy-start | bytes 6148
  245.8 18.6 %copy-start.27 = (f32[384]{0:T(512)}, f32[384]{0:T(512)S(1)}, u32[]{:S(2)}) copy-start(f32[384]{0:T(512)S(1)} %add_rsqrt_fusion.2) | copy-start | bytes 4612
  279.9 113.4 %reduce-scatter.18.cloned.1.call-start = ((), (), s32[]{:S(2)}) async-start(), calls=%async_computation.14 | async-start | bytes 1179648 | tf_op jit(solution)/shard_map/reduce_scatter | solution.py:354
  304.1 152.0 %reduce-scatter.16.cloned.1.call-start = ((), (), s32[]{:S(2)}) async-start(), calls=%async_computation.13 | async-start | bytes 3538944 | tf_op jit(solution)/shard_map/reduce_scatter | solution.py:353
  311.5 24.7 %slice-start = ((s8[6291456]{0:T(1024)(128)(4,1)}), s8[4194304]{0:T(1024)(128)(4,1)S(1)}, s32[]{:S(2)}) async-start(s8[6291456]{0:T(1024)(128)(4,1)} %bitcast.292), calls=%async_computation.22 | async-start | bytes 8388608
  373.3 174.0 %reduce-scatter.24.cloned.1.call-start = ((), (), s32[]{:S(2)}) async-start(), calls=%async_computation.17 | async-start | bytes 4718592 | tf_op jit(solution)/shard_map/reduce_scatter | solution.py:356
  380.6 258.0 %reduce-scatter.20.cloned.1.call-start = ((), (), s32[]{:S(2)}) async-start(), calls=%async_computation.15 | async-start | bytes 4718592 | tf_op jit(solution)/shard_map/reduce_scatter | solution.py:355
  386.6 316.8 %reduce-scatter.32.cloned.1.call-start = ((), (), s32[]{:S(2)}) async-start(), calls=%async_computation.21 | async-start | bytes 294912
  391.0 334.0 %reduce-scatter.30.cloned.1.call-start = ((), (), s32[]{:S(2)}) async-start(), calls=%async_computation.20 | async-start | bytes 163840
  395.0 352.4 %reduce-scatter.28.cloned.1.call-start = ((), (), s32[]{:S(2)}) async-start(), calls=%async_computation.19 | async-start | bytes 327680
  458.5 311.5 %reduce-scatter.26.cloned.1.call-start = ((), (), s32[]{:S(2)}) async-start(), calls=%async_computation.18 | async-start | bytes 327680 | tf_op jit(solution)/shard_map/reduce_scatter | solution.py:369
  549.1 243.5 %reduce-scatter.22.cloned.1.call-start = ((), (), s32[]{:S(2)}) async-start(), calls=%async_computation.16 | async-start | bytes 327680 | tf_op jit(solution)/shard_map/reduce_scatter | solution.py:366
  648.4 145.6 %copy-start.1 = (bf16[8,64,256]{2,1,0:T(8,128)(2,1)S(1)}, bf16[8,64,256]{2,1,0:T(8,128)(2,1)}, u32[]{:S(2)}) copy-start(bf16[8,64,256]{2,1,0:T(8,128)(2,1)} %param.17) | copy-start | bytes 786436
  (43 other events, 226.6 us)
Sparse Core Ops, SparseCore 0:
  16.1 44.6 all-gather.5
  63.0 52.0 all-gather.7
  117.2 48.4 all-gather.9
  280.0 31.4 all-reduce.4
  314.8 63.5 reduce-scatter.17
  382.2 73.8 reduce-scatter.15
  460.2 87.0 reduce-scatter.23
  550.9 87.6 reduce-scatter.19
  642.3 60.9 reduce-scatter.31
  706.3 18.5 reduce-scatter.29
  727.4 19.9 reduce-scatter.27
  749.9 20.0 reduce-scatter.25
  772.5 20.0 reduce-scatter.21
where the time goes:
time: 806 us; the launch traced here: 801 us
  waiting for transfers between devices  324 us (40%)
  matrix products  169 us (21%)
  blocking collectives  140 us (17%)
  local copies, waits for them, and re-layouts  93.5 us (12%)
  other arithmetic  57.5 us (7%)
  between operations  16.3 us (2%)
    unnamed x16, waiting for transfers between devices  83.7 us
    reduce_scatter x1, waiting for transfers between devices, on_device(): lax.psum_scatter(grad_in, 'batch', scatter_dimension=0, tiled=True)  79.9 us
    reduce_scatter x1, waiting for transfers between devices, on_device(): lax.psum_scatter(grad_qkv, 'batch', scatter_dimension=1, tiled=True)  61 us
    reduce_scatter x1, waiting for transfers between devices, on_device(): lax.psum_scatter(grad_down, 'batch', scatter_dimension=1, tiled=True)  55.1 us
    all_gather x1, blocking collectives, on_device(): lax.all_gather(part_out, 'batch', axis=0, tiled=True)  34.6 us
    psum x1, blocking collectives, on_device(): state_summary, total = lax.psum((summary_part, total_part), 'seq')  33.7 us
    dot_general x1, matrix products, on_device(): upper = jnp.dot(normed_two, w_in, preferred_element_type=wider_number_type)  33.6 us
    reduce_scatter x1, waiting for transfers between devices, on_device(): lax.psum_scatter(first_in.astype(jnp.bfloat16), 'seq', scatter_dimension=...  21.1 us
  transfers between devices with their start and end apart: 13, of which 9 were waited for; matrix products, arithmetic and copies ran while one was open for 36% of the time, Pallas kernels for 0%

commit v1 on v0

--- a/solution.py
+++ b/solution.py
@@ -1,6 +1,10 @@
+import functools
+
 import jax
 import jax.numpy as jnp
 from jax import lax
+from jax.experimental import pallas as pl
+from jax.experimental.pallas import tpu as pltpu
 from jax.sharding import PartitionSpec as P
 
 SHORT = 1024
@@ -376,7 +380,867 @@
     return (result[None], tokens_grad[None], owned[0], owned[1], owned[2], owned[3], owned[4])
 
 
+MESH = pl.DeviceIdType.MESH
+LOW = jnp.bfloat16
+WIDE = jnp.float32
+LOG2E = 1.4426950408889634
+ROOT_HALF = 0.7071067811865476
+PDF_SCALE = 0.3989422804014327
+PAD = 16
+
+
+def dot_over(a, b, ca, cb):
+    return lax.dot_general(a, b, (((ca,), (cb,)), ((), ())), preferred_element_type=WIDE)
+
+
+def nn(a, b):
+    return dot_over(a, b, 1, 0)
+
+
+def nt(a, b):
+    return dot_over(a, b, 1, 1)
+
+
+def turn(a):
+    if a.dtype == LOW:
+        return a.astype(WIDE).T.astype(LOW)
+    return a.T
+
+
+def flat(a):
+    return a.reshape(-1, a.shape[-1])
+
+
+def unit_norm(x):
+    cen = x - jnp.mean(x, axis=-1, keepdims=True)
+    inv = lax.rsqrt(jnp.mean(cen * cen, axis=-1, keepdims=True) + EPS)
+    return cen * inv, inv
+
+
+def norm_back(incoming, unit, inv, gain):
+    e = incoming * gain
+    mean_e = jnp.mean(e, axis=-1, keepdims=True)
+    mean_eu = jnp.mean(e * unit, axis=-1, keepdims=True)
+    return inv * (e - mean_e - unit * mean_eu)
+
+
+def features(proj, u_low, scale, feat):
+    wide = u_low.astype(WIDE)
+    sq = jnp.sum(wide * wide, axis=0, keepdims=True)
+    shift = (0.5 * scale * scale * LOG2E) * sq
+    half_log = 0.5 * (feat.bit_length() - 1)
+    return jnp.exp2((scale * LOG2E) * proj - (shift + half_log))
+
+
+class Wires:
+    def __init__(self, send_sems, recv_sems):
+        self.send_sems, self.recv_sems, self.used, self.sent = send_sems, recv_sems, 0, []
+
+    def send(self, src, dst, dev):
+        c = pltpu.make_async_remote_copy(
+            src_ref=src,
+            dst_ref=dst,
+            send_sem=self.send_sems.at[self.used],
+            recv_sem=self.recv_sems.at[self.used],
+            device_id=dev,
+            device_id_type=MESH,
+        )
+        self.used += 1
+        c.start()
+        self.sent.append(c)
+        return c
+
+    def left(self, copies):
+        for c in copies:
+            c.wait_send()
+            self.sent = [o for o in self.sent if o is not c]
+
+    def drain(self):
+        self.left(list(self.sent))
+
+
+def arrived(copies):
+    for c in copies:
+        c.wait_recv()
+
+
+def layer_kernel(
+    nz,
+    ns,
+    tok,
+    wqkv_in,
+    wo_in,
+    win_in,
+    wdn_in,
+    nrm_in,
+    rf,
+    ls,
+    pos,
+    cnt,
+    mg,
+    mixed_out,
+    tgrad_out,
+    gqkv,
+    gop,
+    gin,
+    gdn,
+    gnorm,
+    w0,
+    w1,
+    w2,
+    nb,
+    wkvt,
+    wqt,
+    wo,
+    xnt,
+    kvt,
+    vs,
+    kft,
+    pm,
+    pt,
+    posc,
+    rft,
+    sumf,
+    loc,
+    ar_a,
+    ar_r1,
+    ar_r2,
+    ar_f,
+    dsumt,
+    qrt,
+    qfr,
+    num_r,
+    den_r,
+    dn_st,
+    hot,
+    hort,
+    dmid_low,
+    xnrt,
+    dqt,
+    dhd,
+    dxqt,
+    gkv,
+    gqo,
+    g1,
+    g2,
+    rc_kv,
+    rc_qo,
+    rc1,
+    rc2,
+    ra_kv,
+    ra_qo,
+    ra1,
+    ra2,
+    rb_kv,
+    rb_qo,
+    rb1,
+    rb2,
+    rz_kv,
+    rz_qo,
+    rz1,
+    rz2,
+    ng_a,
+    ng_r,
+    mixed_v,
+    tgrad_v,
+    send_sems,
+    recv_sems,
+    out_sems,
+):
+    rows, width = tok.shape
+    slots = mg.shape[0]
+    heads, size, feat = rf.shape
+    scale = size**-0.25
+    bd = w0.shape[3]
+    sw = wqkv_in.shape[2]
+    fw = w1.shape[4]
+    tile = 256
+    wide_tile = 512
+    b = lax.axis_index("batch")
+    s = lax.axis_index("seq")
+    x = lax.rem(b, 2)
+    z = b // 2
+    c = lax.rem(s, 2)
+    y = s // 2
+    to_core = (b, s + 1 - 2 * c)
+    to_y = (b, s + 2 - 4 * y)
+    to_x = (b + 1 - 2 * x, s)
+    to_z = [(lax.rem(z + k, nz) * 2 + x, s) for k in range(1, nz)]
+    s_core = s + 1 - 2 * c
+    s_y = s + 2 - 4 * y
+    wires = Wires(send_sems, recv_sems)
+
+    w0[s, z, x, :, 0:sw] = wqkv_in[1]
+    w0[s, z, x, :, sw : 2 * sw] = wqkv_in[2]
+    w0[s, z, x, :, 2 * sw : 3 * sw] = wqkv_in[0]
+    w0[s, z, x, :, 3 * sw : 4 * sw] = wo_in[...]
+    w1[s, z, x] = win_in[...]
+    w2[s, z, x] = turn(wdn_in[...])
+    place = (
+        lax.broadcasted_iota(jnp.int32, (bd, 2 * bd), 1)
+        == lax.broadcasted_iota(jnp.int32, (bd, 2 * bd), 0) + bd * x
+    )
+    nb[s, z, x] = nn(
+        jnp.broadcast_to(nrm_in[...], (PAD, bd)), jnp.where(place, 1.0, 0.0).astype(LOW)
+    ).astype(LOW)
+
+    barrier = pltpu.get_barrier_semaphore()
+    partners = [to_core, to_y, to_x] + to_z
+    for dev in partners:
+        pl.semaphore_signal(barrier, inc=1, device_id=dev, device_id_type=MESH)
+    pl.semaphore_wait(barrier, len(partners))
+
+    def spread_z(ref):
+        return [wires.send(ref.at[s, z, x], ref.at[s, z, x], dev) for dev in to_z]
+
+    def spread_z_half(ref, lo, hi):
+        at = ref.at[s, z, x, :, lo:hi]
+        return [wires.send(at, at, dev) for dev in to_z]
+
+    n_z = spread_z(nb)
+    kv_z = spread_z_half(w0, 0, 2 * sw)
+
+    seq_pos = s * rows
+    long_from = ls[0, 0]
+    long_to = long_from + ns * rows - SHORT
+
+    def shared_mask(position):
+        at = position + seq_pos
+        return jnp.where((at >= long_from) & (at < long_to), 1.0, 0.0)
+
+    pos_row = pos[...]
+    posc[...] = jnp.broadcast_to(pos_row.astype(WIDE), (128, slots)).T
+    sh_r = shared_mask(pos_row)
+
+    def select_tile(t, carry):
+        at = pl.multiple_of(t * tile, tile)
+        row_id = lax.broadcasted_iota(jnp.int32, (tile, slots), 0) + at
+        pt[pl.ds(at, tile), :] = jnp.where(row_id == pos_row, 1.0, 0.0).astype(LOW)
+        for j in range(tile // 128):
+            lane = lax.broadcasted_iota(jnp.int32, (slots, 128), 1) + (at + 128 * j)
+            pm[:, pl.ds(at + 128 * j, 128)] = jnp.where(
+                lane.astype(WIDE) == posc[...], 1.0, 0.0
+            ).astype(LOW)
+        lane = lax.broadcasted_iota(jnp.int32, (1, tile), 1) + at
+        sh = shared_mask(lane)
+        row = lax.broadcasted_iota(jnp.int32, (PAD, tile), 0)
+        ones = jnp.where(row == 0, sh, jnp.where(row == 1, 1.0 - sh, 0.0)).astype(LOW)
+        for h in range(heads):
+            vs[h, 2 * size : 2 * size + PAD, pl.ds(at, tile)] = ones
+        return carry
+
+    lax.fori_loop(0, rows // tile, select_tile, 0)
+    for h in range(heads):
+        rft[h] = turn(rf[h])
+
+    arrived(n_z)
+    at = nb.at[s, :, x]
+    n_x = [wires.send(at, at, to_x)]
+    toks_r = nn(pm[...], tok[...])
+    arrived(n_x)
+    at = nb.at[s]
+    n_y = [wires.send(at, at, to_y)]
+    unit_r, _ = unit_norm(toks_r)
+    arrived(n_y)
+    n_c = []
+    for side in (s, s_y):
+        at = nb.at[side]
+        n_c.append(wires.send(at, at, to_core))
+    arrived(kv_z)
+    at = w0.at[s, :, x, :, 0 : 2 * sw]
+    kv_x = [wires.send(at, at, to_x)]
+    qo_z = spread_z_half(w0, 2 * sw, 4 * sw)
+    arrived(n_c)
+
+    def norm_row(i):
+        return jnp.concatenate(
+            [
+                (nb[i, j, 0, 0:1, :] + nb[i, j, 1, 0:1, :]).astype(WIDE)
+                for j in range(nz)
+            ],
+            axis=1,
+        )
+
+    gain1, bias1, gain2, bias2 = [norm_row(i) for i in range(4)]
+    xn_r = (unit_r * gain1 + bias1).astype(LOW)
+    xnrt[...] = turn(xn_r)
+
+    def norm_tile(t, carry):
+        at = pl.multiple_of(t * tile, tile)
+        unit, _ = unit_norm(tok[pl.ds(at, tile), :].astype(WIDE))
+        xnt[:, pl.ds(at, tile)] = turn((unit * gain1 + bias1).astype(LOW))
+        return carry
+
+    lax.fori_loop(0, rows // tile, norm_tile, 0)
+
+    arrived(kv_x)
+    at = w0.at[s, :, :, :, 0 : 2 * sw]
+    kv_y = [wires.send(at, at, to_y)]
+    kv_c = [wires.send(at, at, to_core)]
+    w1_z = spread_z(w1)
+
+    def kv_block(sd):
+        wkvt[sd] = turn(flat(w0[sd, :, :, :, 0 : 2 * sw]))
+
+        def step(t, carry):
+            at = pl.multiple_of(t * wide_tile, wide_tile)
+            cols = pl.ds(at, wide_tile)
+            r = nn(wkvt[sd], xnt[:, cols]).astype(LOW)
+            kvt[sd, :, cols] = r
+            lane = lax.broadcasted_iota(jnp.int32, (1, wide_tile), 1) + at
+            sh = shared_mask(lane).astype(LOW)
+            for i in range(2):
+                h = 2 * sd + i
+                k_h = r[size * i : size * (i + 1)]
+                v_h = r[sw + size * i : sw + size * (i + 1)]
+                kft[h, :, cols] = features(nn(rft[h], k_h), k_h, scale, feat).astype(LOW)
+                vs[h, 0:size, cols] = v_h * sh
+                vs[h, size : 2 * size, cols] = v_h * (1.0 - sh)
+            return carry
+
+        lax.fori_loop(0, rows // wide_tile, step, 0)
+        for i in range(2):
+            h = 2 * sd + i
+            part = nt(vs[h], kft[h]).astype(LOW)
+            ar_a[sd, i, 0:size, :] = part[0:size]
+            ar_a[sd, i, size : size + PAD, :] = part[2 * size :]
+            loc[h] = part[size:]
+
+    arrived(kv_c)
+
+    def kv_first(j, carry):
+        kv_block(s + j * (s_core - s))
+        return carry
+
+    lax.fori_loop(0, 2, kv_first, 0)
+
+    arrived(qo_z)
+    at = w0.at[s, :, x, :, 2 * sw : 4 * sw]
+    qo_x = [wires.send(at, at, to_x)]
+    arrived(kv_y)
+    at = w0.at[s_y, :, :, :, 0 : 2 * sw]
+    kv_c2 = [wires.send(at, at, to_core)]
+    arrived(w1_z)
+    w2_z = spread_z(w2)
+    at = w1.at[s, :, x]
+    w1_x = [wires.send(at, at, to_x)]
+    arrived(kv_c2)
+
+    def kv_second(j, carry):
+        base = s_y
+        kv_block(base + j * (s_core - s))
+        return carry
+
+    lax.fori_loop(0, 2, kv_second, 0)
+
+    def reduce_first(buf, r1):
+        return [
+            wires.send(buf.at[2 * yy + 1 - c], r1.at[yy], to_core) for yy in range(2)
+        ]
+
+    def reduce_second(buf, r1, r2, f, copies):
+        arrived(copies)
+        wires.left(copies)
+        for yy in range(2):
+            mine = 2 * yy + c
+            buf[mine] = (buf[mine].astype(WIDE) + r1[yy].astype(WIDE)).astype(LOW)
+        return [wires.send(buf.at[2 * yy + c], r2.at[yy], to_y) for yy in range(2)]
+
+    def reduce_third(buf, r1, r2, f, copies):
+        arrived(copies)
+        wires.left(copies)
+        for yy in range(2):
+            mine = 2 * yy + c
+            f[mine] = (buf[mine].astype(WIDE) + r2[yy].astype(WIDE)).astype(LOW)
+        return [wires.send(f.at[2 * yy + c], f.at[2 * yy + c], to_core) for yy in range(2)]
+
+    ar1 = reduce_first(ar_a, ar_r1.at[0])
+    arrived(qo_x)
+    at = w0.at[s, :, :, :, 2 * sw : 4 * sw]
+    qo_c = [wires.send(at, at, to_core)]
+    qo_y = [wires.send(at, at, to_y)]
+    ar1 = reduce_second(ar_a, ar_r1.at[0], ar_r2.at[0], ar_f.at[0], ar1)
+    arrived(w1_x)
+    at = w1.at[s]
+    w1_y = [wires.send(at, at, to_y)]
+    w1_c = [wires.send(at, at, to_core)]
+    arrived(w2_z)
+    at = w2.at[s, :, x]
+    w2_x = [wires.send(at, at, to_x)]
+    arrived(qo_y)
+    at = w0.at[s_y, :, :, :, 2 * sw : 4 * sw]
+    qo_c2 = [wires.send(at, at, to_core)]
+    ar1 = reduce_third(ar_a, ar_r1.at[0], ar_r2.at[0], ar_f.at[0], ar1)
+    arrived(qo_c)
+    arrived(qo_c2)
+    for i in range(ns):
+        wqt[sw * i : sw * (i + 1), :] = turn(flat(w0[i, :, :, :, 2 * sw : 3 * sw]))
+        wo[:, sw * i : sw * (i + 1)] = flat(w0[i, :, :, :, 3 * sw : 4 * sw])
+
+    qr = nn(wqt[...], xnrt[...]).astype(LOW)
+    for h in range(heads):
+        q_h = qr[size * h : size * (h + 1)]
+        qrt[h] = q_h
+        qfr[h] = features(nn(rft[h], q_h), q_h, scale, feat).astype(LOW)
+
+    arrived(ar1)
+    for h in range(heads):
+        sumf[h, 0:size, :] = ar_f[0, h // 2, h % 2, 0:size, :]
+        sumf[h, size : 2 * size, :] = loc[h, 0:size, :]
+        first = lax.broadcasted_iota(jnp.int32, (PAD, feat), 0) == 0
+        sumf[h, 2 * size : 2 * size + PAD, :] = jnp.where(
+            first,
+            ar_f[0, h // 2, h % 2, size : size + PAD, :].astype(WIDE),
+            loc[h, size : size + PAD, :].astype(WIDE),
+        ).astype(LOW)
+
+    def split_ratio(nd, sh):
+        pick = jnp.broadcast_to(sh, (size, sh.shape[1])) > 0.5
+        num = jnp.where(pick, nd[0:size], nd[size : 2 * size])
+        den = jnp.where(sh > 0.5, nd[2 * size : 2 * size + 1], nd[2 * size + 1 : 2 * size + 2])
+        return num, den
+
+    for h in range(heads):
+        num, den = split_ratio(nn(sumf[h], qfr[h]), sh_r)
+        num_r[h] = num
+        den_r[h] = jnp.broadcast_to(den, (8, slots))
+        hort[size * h : size * (h + 1), :] = (num * (1.0 / den)).astype(LOW)
+
+    middle_r = toks_r + nn(turn(hort[...]), wo[...])
+    unit2, inv2 = unit_norm(middle_r)
+    xn2_r = (unit2 * gain2 + bias2).astype(LOW)
+    xn2_rt = turn(xn2_r)
+    slot_id = lax.broadcasted_iota(jnp.int32, (slots, 1), 0)
+    cot = mg[...].astype(WIDE) * jnp.where(slot_id < cnt[0, 0], 1.0, 0.0)
+    cot_low = cot.astype(LOW)
+    cot_t = turn(cot_low)
+
+    arrived(w2_x)
+    at = w2.at[s]
+    w2_y = [wires.send(at, at, to_y)]
+    w2_c = [wires.send(at, at, to_core)]
+    arrived(w1_y)
+    at = w1.at[s_y]
+    w1_c2 = [wires.send(at, at, to_core)]
+    arrived(w2_y)
+    at = w2.at[s_y]
+    w2_c2 = [wires.send(at, at, to_core)]
+    arrived(w1_c)
+    arrived(w2_c)
+    arrived(w1_c2)
+    arrived(w2_c2)
+
+    dn2 = jnp.zeros((slots, width), WIDE)
+    for i in range(ns):
+        win = flat(w1[i])
+        upper = nn(xn2_r, win)
+        cdf = 0.5 + 0.5 * lax.erf(upper * ROOT_HALF)
+        act = (upper * cdf).astype(LOW)
+        slope = cdf + upper * (PDF_SCALE * jnp.exp(-0.5 * upper * upper))
+        du = (nn(cot_low, flat(w2[i])) * slope).astype(LOW)
+        g1[i] = nn(xn2_rt, du).astype(LOW).reshape(g1.shape[1:])
+        g2[i] = nn(cot_t, act).astype(LOW).reshape(g2.shape[1:])
+        dn2 = dn2 + nt(du, win)
+
+    def scatter_first(g, rc):
+        return [wires.send(g.at[2 * yy + 1 - c], rc.at[yy], to_core) for yy in range(2)]
+
+    def scatter_add_core(g, rc, copies):
+        arrived(copies)
+        for yy in range(2):
+            def step(j, carry):
+                g[2 * yy + c, j] = (g[2 * yy + c, j].astype(WIDE) + rc[yy, j].astype(WIDE)).astype(LOW)
+                return carry
+            lax.fori_loop(0, nz, step, 0)
+
+    def scatter_y(g, ra):
+        return [wires.send(g.at[2 * (1 - y) + c], ra, to_y)]
+
+    def scatter_y_add(g, ra, copies):
+        arrived(copies)
+        def step(j, carry):
+            g[s, j] = (g[s, j].astype(WIDE) + ra[j].astype(WIDE)).astype(LOW)
+            return carry
+        lax.fori_loop(0, nz, step, 0)
+
+    def scatter_x(g, rb):
+        return [wires.send(g.at[s, :, 1 - x], rb, to_x)]
+
+    def scatter_x_add(g, rb, copies):
+        arrived(copies)
+        g[s, :, x] = (g[s, :, x].astype(WIDE) + rb[...].astype(WIDE)).astype(LOW)
+
+    def scatter_z(g, rz):
+        return [
+            wires.send(g.at[s, lax.rem(z + k, nz), x], rz.at[k - 1], to_z[k - 1])
+            for k in range(1, nz)
+        ]
+
+    def scatter_done(g, rz, copies):
+        arrived(copies)
+        total = g[s, z, x].astype(WIDE)
+        for k in range(nz - 1):
+            total = total + rz[k].astype(WIDE)
+        return total
+
+    s1 = scatter_first(g1, rc1)
+    s2 = scatter_first(g2, rc2)
+
+    norm_g2 = jnp.sum(dn2 * unit2, axis=0, keepdims=True)
+    norm_g3 = jnp.sum(dn2, axis=0, keepdims=True)
+    dm = cot + norm_back(dn2, unit2, inv2, gain2)
+    d_att = dm.astype(LOW)
+    dmid_low[...] = d_att
+    for i in range(ns):
+        part = nn(hort[...], d_att[:, sw * i : sw * (i + 1)]).astype(LOW)
+        gqo[i, :, :, :, sw : 2 * sw] = part.reshape(gqo.shape[1:4] + (sw,))
+    dhd[...] = nt(wo[...], d_att)
+    for h in range(heads):
+        dh = dhd[size * h : size * (h + 1), :]
+        rden = 1.0 / den_r[h, 0:1, :]
+        d_num = (dh * rden).astype(LOW)
+        d_den = (-jnp.sum(dh * num_r[h], axis=0, keepdims=True) * (rden * rden)).astype(LOW)
+        shl = sh_r.astype(LOW)
+        dn_st[h, 0:size, :] = d_num * shl
+        dn_st[h, size : 2 * size, :] = d_num * (1.0 - shl)
+        row = lax.broadcasted_iota(jnp.int32, (PAD, slots), 0)
+        dd = jnp.broadcast_to(d_den.astype(WIDE), (PAD, slots))
+        dn_st[h, 2 * size : 2 * size + PAD, :] = jnp.where(
+            row == 0, dd * sh_r, jnp.where(row == 1, dd * (1.0 - sh_r), 0.0)
+        ).astype(LOW)
+        part = nt(dn_st[h], qfr[h]).astype(LOW)
+        ar_a[h // 2, h % 2, 0:size, :] = part[0:size]
+        ar_a[h // 2, h % 2, size : size + PAD, :] = part[2 * size :]
+        loc[h] = part[size:]
+    ar2 = reduce_first(ar_a, ar_r1.at[1])
+    scatter_add_core(g1, rc1, s1)
+    s1 = scatter_y(g1, ra1)
+    scatter_add_core(g2, rc2, s2)
+    s2 = [wires.send(g2.at[2 * yy + c, :, 1 - x], rb2.at[yy], to_x) for yy in range(2)]
+    ar2 = reduce_second(ar_a, ar_r1.at[1], ar_r2.at[1], ar_f.at[1], ar2)
+
+    for h in range(heads):
+        d_qf = nn(turn(sumf[h]), dn_st[h])
+        w = d_qf * qfr[h].astype(WIDE)
+        ws = jnp.sum(w, axis=0, keepdims=True)
+        q_h = qrt[h].astype(WIDE)
+        dqt[size * h : size * (h + 1), :] = (
+            scale * nn(rf[h], w.astype(LOW)) - (scale * scale) * q_h * ws
+        ).astype(LOW)
+    for i in range(ns):
+        part = nt(xnrt[...], dqt[sw * i : sw * (i + 1), :]).astype(LOW)
+        gqo[i, :, :, :, 0:sw] = part.reshape(gqo.shape[1:4] + (sw,))
+    s0 = scatter_first(gqo, rc_qo)
+    acc = jnp.zeros((width, slots), WIDE)
+    for i in range(ns):
+        acc = acc + nn(flat(w0[i, :, :, :, 2 * sw : 3 * sw]), dqt[sw * i : sw * (i + 1), :])
+    dxqt[...] = acc.astype(LOW)
+    ar2 = reduce_third(ar_a, ar_r1.at[1], ar_r2.at[1], ar_f.at[1], ar2)
+
+    def dense_tile(t):
+        at = pl.multiple_of(t * tile, tile)
+        cols = pl.ds(at, tile)
+        q = nn(wqt[...], xnt[:, cols]).astype(LOW)
+        lane = lax.broadcasted_iota(jnp.int32, (1, tile), 1) + at
+        sh = shared_mask(lane)
+        for h in range(heads):
+            q_h = q[size * h : size * (h + 1)]
+            qf = features(nn(rft[h], q_h), q_h, scale, feat).astype(LOW)
+            num, den = split_ratio(nn(sumf[h], qf), sh)
+            hot[size * h : size * (h + 1), :] = (num * (1.0 / den)).astype(LOW)
+        mid = tok[cols, :].astype(WIDE) + nn(turn(hot[...]), wo[...])
+        unit, _ = unit_norm(mid)
+        xn2 = (unit * gain2 + bias2).astype(LOW)
+        total = mid
+        for i in range(ns):
+            up = nn(xn2, flat(w1[i]))
+            act = (up * (0.5 + 0.5 * lax.erf(up * ROOT_HALF))).astype(LOW)
+            total = total + nt(act, flat(w2[i]))
+        mixed_v[cols, :] = total.astype(LOW)
+
+    def dense_loop(lo, hi):
+        def step(t, carry):
+            dense_tile(t)
+            return carry
+
+        lax.fori_loop(lo, hi, step, 0)
+
+    dense_loop(0, 2)
+
+    arrived(ar2)
+    for h in range(heads):
+        first = lax.broadcasted_iota(jnp.int32, (PAD, feat), 0) == 0
+        tail = jnp.where(
+            first,
+            ar_f[1, h // 2, h % 2, size : size + PAD, :].astype(WIDE),
+            loc[h, size : size + PAD, :].astype(WIDE),
+        ).astype(LOW)
+        stack = jnp.concatenate([ar_f[1, h // 2, h % 2, 0:size, :], loc[h, 0:size, :], tail], axis=0)
+        ar_a[h // 2, h % 2, 0:size, :] = stack[0:size]
+        dsumt[h] = turn(stack)
+
+    scatter_y_add(g1, ra1, s1)
+    s1 = scatter_x(g1, rb1)
+    arrived(s2)
+    for yy in range(2):
+        g2[2 * yy + c, :, x] = (g2[2 * yy + c, :, x].astype(WIDE) + rb2[yy].astype(WIDE)).astype(LOW)
+    s2 = [wires.send(g2.at[2 * (1 - y) + c, :, x], ra2, to_y)]
+
+    def key_block(sd, carry):
+        def step(t, carry2):
+            at = pl.multiple_of(t * wide_tile, wide_tile)
+            cols = pl.ds(at, wide_tile)
+            lane = lax.broadcasted_iota(jnp.int32, (1, wide_tile), 1) + at
+            sh = shared_mask(lane)
+            pick = jnp.broadcast_to(sh, (size, wide_tile)) > 0.5
+            for i in range(2):
+                h = 2 * sd + i
+                kf = kft[h, :, cols]
+                w = nn(dsumt[h], vs[h, :, cols]) * kf.astype(WIDE)
+                ws = jnp.sum(w, axis=0, keepdims=True)
+                k_h = kvt[sd, size * i : size * (i + 1), cols].astype(WIDE)
+                dk = scale * nn(rf[h], w.astype(LOW)) - (scale * scale) * k_h * ws
+                dva = nn(ar_a[sd, i, 0:size, :], kf)
+                dvb = nn(loc[h, 0:size, :], kf)
+                kvt[sd, size * i : size * (i + 1), cols] = dk.astype(LOW)
+                kvt[sd, sw + size * i : sw + size * (i + 1), cols] = jnp.where(pick, dva, dvb).astype(LOW)
+            return carry2
+
+        lax.fori_loop(0, rows // wide_tile, step, 0)
+        gkv[sd] = nt(xnt[...], kvt[sd]).astype(LOW).reshape(gkv.shape[1:])
+        return carry
+
+    lax.fori_loop(0, ns, key_block, 0)
+    s3 = scatter_first(gkv, rc_kv)
+    scatter_add_core(gqo, rc_qo, s0)
+    s0 = scatter_y(gqo, ra_qo)
+    scatter_x_add(g1, rb1, s1)
+    s1 = scatter_z(g1, rz1)
+    arrived(s2)
+    g2[s, :, x] = (g2[s, :, x].astype(WIDE) + ra2[...].astype(WIDE)).astype(LOW)
+    s2 = scatter_z(g2, rz2)
+    scatter_add_core(gkv, rc_kv, s3)
+    s3 = scatter_y(gkv, ra_kv)
+
+    ng_a[...] = jnp.zeros(ng_a.shape, WIDE)
+
+    def token_tile(t, carry):
+        at = pl.multiple_of(t * tile, tile)
+        cols = pl.ds(at, tile)
+        dxt = nn(dxqt[...], pm[:, cols])
+        for i in range(ns):
+            dxt = dxt + nn(flat(w0[i, :, :, :, 0 : 2 * sw]), kvt[i, :, cols])
+        dx = dxt.T
+        unit, inv = unit_norm(tok[cols, :].astype(WIDE))
+        tgrad_v[cols, :] = norm_back(dx, unit, inv, gain1) + nn(pt[cols, :], dmid_low[...])
+        ng_a[0:1, :] += jnp.sum(dx * unit, axis=0, keepdims=True)
+        ng_a[1:2, :] += jnp.sum(dx, axis=0, keepdims=True)
+        return carry
+
+    lax.fori_loop(0, rows // tile, token_tile, 0)
+    out_t = pltpu.make_async_copy(tgrad_v, tgrad_out, out_sems.at[0])
+    out_t.start()
+    ng_a[2:3, :] = norm_g2
+    ng_a[3:4, :] = norm_g3
+
+    n_g = [wires.send(ng_a, ng_r.at[0], to_core)]
+    scatter_y_add(gqo, ra_qo, s0)
+    s0 = scatter_x(gqo, rb_qo)
+    scatter_y_add(gkv, ra_kv, s3)
+    s3 = scatter_x(gkv, rb_kv)
+    arrived(n_g)
+    wires.left(n_g)
+    ng_a[...] += ng_r[0]
+    n_g = [wires.send(ng_a, ng_r.at[1], to_y)]
+    dense_loop(2, 4)
+    arrived(n_g)
+    wires.left(n_g)
+    ng_a[...] += ng_r[1]
+    n_g = [wires.send(ng_a, ng_r.at[2], to_x)]
+    scatter_x_add(gqo, rb_qo, s0)
+    s0 = scatter_z(gqo, rz_qo)
+    scatter_x_add(gkv, rb_kv, s3)
+    s3 = scatter_z(gkv, rz_kv)
+    arrived(n_g)
+    wires.left(n_g)
+    ng_a[...] += ng_r[2]
+    n_g = [wires.send(ng_a, ng_r.at[2 + k], to_z[k - 1]) for k in range(1, nz)]
+    dense_loop(4, rows // tile)
+    out_m = pltpu.make_async_copy(mixed_v, mixed_out, out_sems.at[1])
+    out_m.start()
+
+    gin[...] = scatter_done(g1, rz1, s1)
+    gdn[...] = scatter_done(g2, rz2, s2).T
+    qo = scatter_done(gqo, rz_qo, s0)
+    kv = scatter_done(gkv, rz_kv, s3)
+    gqkv[0] = qo[:, 0:sw]
+    gqkv[1] = kv[:, 0:sw]
+    gqkv[2] = kv[:, sw : 2 * sw]
+    gop[...] = qo[:, sw : 2 * sw]
+    arrived(n_g)
+    total = ng_a[...]
+    for k in range(1, nz):
+        total = total + ng_r[2 + k]
+    row = lax.broadcasted_iota(jnp.int32, total.shape, 0)
+    mine = jnp.sum(jnp.where(row == s, total, 0.0), axis=0, keepdims=True)
+    mine = jnp.broadcast_to(mine, total.shape)
+    gnorm[...] = pltpu.roll(mine, lax.rem(width - bd * b, width), 1)[0:1, 0:bd]
+    wires.drain()
+    out_t.wait()
+    out_m.wait()
+
+
+def fits(mesh, args):
+    tokens, qkv_weight, _, in_weight, _, _, rand_features = args[:7]
+    nbat, ns = mesh.shape["batch"], mesh.shape["seq"]
+    bd, sw = qkv_weight.shape[1], qkv_weight.shape[2]
+    rows, width = tokens.shape[1], tokens.shape[2]
+    heads, size, feat = rand_features.shape
+    return (
+        ns == 4
+        and nbat == 8
+        and tokens.shape[0] == 1
+        and bd % 64 == 0
+        and sw == 2 * size
+        and in_weight.shape[1] == 4 * sw
+        and heads == 2 * ns
+        and rows % 512 == 0
+        and feat == 256
+    )
+
+
+def fused_layer(
+    nbat,
+    ns,
+    tokens,
+    qkv_weight,
+    out_proj,
+    in_weight,
+    out_weight,
+    norm_params,
+    rand_features,
+    long_start,
+    masked_pos,
+    masked_count,
+    masked_grad,
+):
+    nz = nbat // 2
+    rows, width = tokens.shape[1], tokens.shape[2]
+    slots = masked_grad.shape[1]
+    heads, size, feat = rand_features.shape
+    bd, sw = qkv_weight.shape[1], qkv_weight.shape[2]
+    fw = in_weight.shape[1]
+    stack = 2 * size + PAD
+    low = lambda *shape: pltpu.VMEM(shape, LOW)
+    wide = lambda *shape: pltpu.VMEM(shape, WIDE)
+    vmem = pl.BlockSpec(memory_space=pltpu.VMEM)
+    smem = pl.BlockSpec(memory_space=pltpu.SMEM)
+    anywhere = pl.BlockSpec(memory_space=pl.ANY)
+    tall = (nz, 2, bd)
+    scratch = [
+        low(ns, *tall, 4 * sw),
+        low(ns, *tall, fw),
+        low(ns, *tall, fw),
+        low(ns, nz, 2, PAD, 2 * bd),
+        low(ns, 2 * sw, width),
+        low(width, width),
+        low(width, width),
+        low(width, rows),
+        low(ns, 2 * sw, rows),
+        low(heads, stack, rows),
+        low(heads, feat, rows),
+        low(slots, rows),
+        low(rows, slots),
+        wide(slots, 128),
+        low(heads, feat, size),
+        low(heads, stack, feat),
+        low(heads, size + PAD, feat),
+        low(ns, 2, size + PAD, feat),
+        low(2, 2, 2, size + PAD, feat),
+        low(2, 2, 2, size + PAD, feat),
+        low(2, ns, 2, size + PAD, feat),
+        low(heads, feat, stack),
+        low(heads, size, slots),
+        low(heads, feat, slots),
+        wide(heads, size, slots),
+        wide(heads, 8, slots),
+        low(heads, stack, slots),
+        low(width, 256),
+        low(width, slots),
+        low(slots, width),
+        low(width, slots),
+        low(width, slots),
+        wide(width, slots),
+        low(width, slots),
+        low(ns, *tall, 2 * sw),
+        low(ns, *tall, 2 * sw),
+        low(ns, *tall, fw),
+        low(ns, *tall, fw),
+        low(2, *tall, 2 * sw),
+        low(2, *tall, 2 * sw),
+        low(2, *tall, fw),
+        low(2, *tall, fw),
+        low(*tall, 2 * sw),
+        low(*tall, 2 * sw),
+        low(*tall, fw),
+        low(nz, bd, fw),
+        low(nz, bd, 2 * sw),
+        low(nz, bd, 2 * sw),
+        low(nz, bd, fw),
+        low(2, nz, bd, fw),
+        low(nz - 1, bd, 2 * sw),
+        low(nz - 1, bd, 2 * sw),
+        low(nz - 1, bd, fw),
+        low(nz - 1, bd, fw),
+        wide(8, width),
+        wide(2 + nz, 8, width),
+        low(rows, width),
+        wide(rows, width),
+        pltpu.SemaphoreType.DMA((96,)),
+        pltpu.SemaphoreType.DMA((96,)),
+        pltpu.SemaphoreType.DMA((2,)),
+    ]
+    f32 = lambda *shape: jax.ShapeDtypeStruct(shape, WIDE)
+    outs = pl.pallas_call(
+        functools.partial(layer_kernel, nz, ns),
+        out_shape=(
+            jax.ShapeDtypeStruct((rows, width), LOW),
+            f32(rows, width),
+            f32(3, bd, sw),
+            f32(bd, sw),
+            f32(bd, fw),
+            f32(fw, bd),
+            f32(1, bd),
+        ),
+        in_specs=[vmem] * 7 + [smem, vmem, smem, vmem],
+        out_specs=(anywhere, anywhere, vmem, vmem, vmem, vmem, vmem),
+        scratch_shapes=scratch,
+        compiler_params=pltpu.CompilerParams(
+            collective_id=0, has_side_effects=True, vmem_limit_bytes=62 * 2**20
+        ),
+        name="layer",
+    )(
+        tokens.reshape(rows, width),
+        qkv_weight,
+        out_proj,
+        in_weight,
+        out_weight,
+        norm_params,
+        rand_features,
+        long_start.reshape(1, 1),
+        masked_pos,
+        masked_count,
+        masked_grad.reshape(slots, width),
+    )
+    return (outs[0][None], outs[1][None]) + outs[2:]
+
+
 def solution(mesh):
+    def body(*args):
+        if fits(mesh, args):
+            return fused_layer(mesh.shape["batch"], mesh.shape["seq"], *args)
+        return on_device(*args)
+
     placed = (
         P("batch", "seq", None),
         P(None, "batch", "seq"),
@@ -391,7 +1255,7 @@
         P("batch", "seq", None),
     )
     return jax.shard_map(
-        on_device,
+        body,
         mesh=mesh,
         in_specs=placed,
         out_specs=(

time: 806 us -> 162 us (0.20)
  waiting for transfers between devices: 324 us -> 0 us
  matrix products: 169 us -> 0 us
  Pallas kernels: 0 us -> 150 us
  blocking collectives: 140 us -> 0 us
  local copies, waits for them, and re-layouts: 93.5 us -> 10.2 us
  other arithmetic: 57.5 us -> 0 us
  between operations: 16.3 us -> 1.95 us
    reduce_scatter x6 -> x0, waiting for transfers between devices: 238 us -> none  [the longest x1 79.9 us: on_device(): lax.psum_scatter(grad_in, 'batch', scatter_dimension=0, tiled=True)]
    dot_general x42 -> x0, matrix products: 169 us -> none  [the longest x1 33.6 us: on_device(): upper = jnp.dot(normed_two, w_in, preferred_element_type=wider_number_type)]
    pallas_call x0 -> x1, Pallas kernels: none -> 150 us  [fused_layer(): pl.pallas_call(functools.partial(layer_kernel, nz, ns), out_shape=(jax.Sh...]
    all_gather x7 -> x0, blocking collectives: 89.3 us -> none  [the longest x1 34.6 us: on_device(): lax.all_gather(part_out, 'batch', axis=0, tiled=True)]
    unnamed x16 -> x0, waiting for transfers between devices: 83.7 us -> none
    psum x2 -> x0, blocking collectives: 44.6 us -> none  [the longest x1 33.7 us: on_device(): state_summary, total = lax.psum((summary_part, total_part), 'seq')]
    gather x12 -> x0, local copies, waits for them, and re-layouts: 36.5 us -> none  [the longest x2 6.89 us: on_device(): query_feat_rows = query_feature_map[picked]]
    reduce_sum x9 -> x0, other arithmetic: 16.3 us -> none  [the longest x1 4.3 us: layer_norm_back(): jnp.sum(incoming * unit_rows, axis=0)]
  transfers between devices with their start and end apart: 13 -> 0, of which waited for: 9 -> 0; matrix products, arithmetic and copies ran while one was open for 36% -> 0% of each run, Pallas kernels for 0% -> 0%
where the time goes in v1:
time: 162 us
  Pallas kernels  150 us (93%)
  local copies, waits for them, and re-layouts  10.2 us (6%)
  between operations  1.95 us (1%)
    pallas_call x1, Pallas kernels, fused_layer(): pl.pallas_call(functools.partial(layer_kernel, nz, ns), out_shape=(jax.Sh...  150 us
    unnamed x18, local copies, waits for them, and re-layouts  10.2 us

profile of v1, /device:TPU:0, one launch (start us, length us, event | category | flops | bytes accessed | tf_op | source)
XLA Modules:
  0.0 162.0 jit_solution(7480864918814180571)
XLA Ops:
  1.9 1.6 copy.18.wdn_in
  3.5 149.8 %layer.1 = (bf16[1536,512]{1,0:T(8,128)(2,1)}, f32[1536,512]{1,0:T(8,128)}, f32[3,64,128]{2,1,0:T(8,128)}, f32[64,128]{1,0:T(8,128)}, f32[64,512]{1,0:T(8,128)}, /*index=5*/f32[512,64]{1,0:T(8,128)}, f32[1,64]{1,0:T(1,128)}) custom-call(bf16[1536,512]{1,0:T(8,128)(2,1)} %bitcast.8, bf16[3,64,128]{2,1,0:T(8,128)(2,1)} %wqkv_in.1, bf16[64,128]{1,0:T(8,128)(2,1)} %wo_in.1, ...), custom_call_target="tpu_custom_call" | custom-call | tf_op jit(solution)/shard_map/layer/pallas_call | solution.py:1204
  153.3 1.7 %copy.19 = f32[512,64]{0,1:T(8,128)} copy(f32[512,64]{1,0:T(8,128)} %get-tuple-element.26) | data formatting | bytes 262144
  155.0 0.0 copy-start
  155.0 2.8 %copy.28 = bf16[1,1536,512]{2,1,0:T(8,128)(2,1)} copy(bf16[1,1536,512]{2,1,0:T(8,128)(2,1)} %bitcast.7) | data formatting | bytes 3145728
  157.8 0.0 copy-done
  157.8 0.0 copy-start.2
  157.8 0.0 copy-start.3
  157.8 0.0 copy-start.1
  157.9 0.0 copy-start.4
  157.9 1.7 %copy.29 = f32[1,1536,512]{2,1,0:T(8,128)} copy(f32[1,1536,512]{2,1,0:T(8,128)S(1)} %bitcast.6) | data formatting | bytes 6291456
  159.5 0.0 copy-done.2
  159.5 0.6 copy.30
  160.2 0.0 copy-done.3
  160.2 0.6 copy.31
  160.8 0.0 copy-done.1
  160.8 0.7 copy.32
  161.5 0.0 copy-done.4
  161.5 0.5 copy.33
Async XLA Ops:
  155.0 2.8 %copy-start = (f32[1536,512]{1,0:T(8,128)S(1)}, f32[1536,512]{1,0:T(8,128)}, u32[]{:S(2)}) copy-start(f32[1536,512]{1,0:T(8,128)} %get-tuple-element.15) | copy-start | bytes 9437188
  157.8 1.7 %copy-start.2 = (f32[3,64,128]{2,1,0:T(8,128)S(1)}, f32[3,64,128]{2,1,0:T(8,128)}, u32[]{:S(2)}) copy-start(f32[3,64,128]{2,1,0:T(8,128)} %get-tuple-element.37) | copy-start | bytes 294916
  157.8 2.3 %copy-start.3 = (f32[64,128]{1,0:T(8,128)S(1)}, f32[64,128]{1,0:T(8,128)}, u32[]{:S(2)}) copy-start(f32[64,128]{1,0:T(8,128)} %get-tuple-element.38) | copy-start | bytes 98308
  157.8 2.9 %copy-start.1 = (f32[64,512]{1,0:T(8,128)S(1)}, f32[64,512]{1,0:T(8,128)}, u32[]{:S(2)}) copy-start(f32[64,512]{1,0:T(8,128)} %get-tuple-element.39) | copy-start | bytes 393220
  157.9 3.6 %copy-start.4 = (f32[1,64]{1,0:T(1,128)S(1)}, f32[1,64]{1,0:T(1,128)}, u32[]{:S(2)}) copy-start(f32[1,64]{1,0:T(1,128)} %get-tuple-element.41) | copy-start | bytes 772

commit v2 on v1

--- a/solution.py
+++ b/solution.py
@@ -387,6 +387,65 @@
 ROOT_HALF = 0.7071067811865476
 PDF_SCALE = 0.3989422804014327
 PAD = 16
+OWN_STEP = {"zxy": (3, 4, 5, 6), "zyx": (4, 5, 4, 5), "plane": (2, 3, 4, 5)}
+KIND = {"kv": "plane", "qo": "zxy", "w1a": "zxy", "w1b": "zyx", "w2a": "zyx", "w2b": "zxy"}
+EARLY = 2
+PLAN = (
+    ("norm", "kv", ),
+    (),
+    (),
+    (),
+    (),
+    ("qo", ),
+    ("w1b", ),
+    ("kv", ),
+    ("w1a", ),
+    ("w2a", "qo", ),
+    ("w2b", "w1b", ),
+    ("kv", "qo", ),
+    ("w1a", "w1b", ),
+    ("qo", ),
+    ("w2a", ),
+    ("ar1", ),
+    ("w2b", ),
+    ("ar1", ),
+    ("w1a", "w2a", ),
+    ("ar1", "w1a", "w1b", "w2b", ),
+    ("w2b", ),
+    ("w1b", ),
+    (),
+    ("w2a", ),
+    (),
+    (),
+    ("w1a", ),
+    ("w1a", ),
+    (),
+    ("g2a", "g2b", "g1a", "g1b", ),
+    (),
+    ("ar2", ),
+    (),
+    ("ar2", "g2a", "g2b", "g1a", "g1b", ),
+    ("qog", ),
+    ("qog", ),
+    (),
+    (),
+    (),
+    (),
+    ("g2a", "g2b", "g1a", ),
+    ("kg", "vg", ),
+    ("g1b", ),
+    (),
+    ("g2b", "qog", ),
+    ("kg", "vg", ),
+    ("g2a", "g1a", "g1b", ),
+    ("vg", "g2b", ),
+    ("qog", ),
+    ("ngs", ),
+    ("kg", "vg", "ngs", ),
+    ("ngs", ),
+    ("kg", "g2a", "ngs", "g1a", ),
+    ("vg", "g1b", "ngs", ),
+)
 
 
 def dot_over(a, b, ca, cb):
@@ -467,7 +526,7 @@
 def layer_kernel(
     nz,
     ns,
-    tok,
+    tok_in,
     wqkv_in,
     wo_in,
     win_in,
@@ -485,6 +544,7 @@
     gin,
     gdn,
     gnorm,
+    tok,
     w0,
     w1,
     w2,
@@ -497,7 +557,6 @@
     vs,
     kft,
     pm,
-    pt,
     posc,
     rft,
     sumf,
@@ -519,26 +578,9 @@
     dqt,
     dhd,
     dxqt,
-    gkv,
-    gqo,
+    g0,
     g1,
     g2,
-    rc_kv,
-    rc_qo,
-    rc1,
-    rc2,
-    ra_kv,
-    ra_qo,
-    ra1,
-    ra2,
-    rb_kv,
-    rb_qo,
-    rb1,
-    rb2,
-    rz_kv,
-    rz_qo,
-    rz1,
-    rz2,
     ng_a,
     ng_r,
     mixed_v,
@@ -546,6 +588,7 @@
     send_sems,
     recv_sems,
     out_sems,
+    *scatter_refs,
 ):
     rows, width = tok.shape
     slots = mg.shape[0]
@@ -553,7 +596,6 @@
     scale = size**-0.25
     bd = w0.shape[3]
     sw = wqkv_in.shape[2]
-    fw = w1.shape[4]
     tile = 256
     wide_tile = 512
     b = lax.axis_index("batch")
@@ -562,20 +604,31 @@
     z = b // 2
     c = lax.rem(s, 2)
     y = s // 2
-    to_core = (b, s + 1 - 2 * c)
-    to_y = (b, s + 2 - 4 * y)
+    s_core = s + 1 - 2 * c
+    s_y = s + 2 - 4 * y
+    s_far = s_core + 2 - 4 * y
+    to_core = (b, s_core)
+    to_y = (b, s_y)
     to_x = (b + 1 - 2 * x, s)
     to_z = [(lax.rem(z + k, nz) * 2 + x, s) for k in range(1, nz)]
-    s_core = s + 1 - 2 * c
-    s_y = s + 2 - 4 * y
+    to_diag = [(lax.rem(z + k, nz) * 2 + 1 - x, s) for k in range(1, nz)]
+    to_plane = to_z + [to_x] + to_diag
+    to_seq = [to_core, to_y, (b, s_far)]
     wires = Wires(send_sems, recv_sems)
+
+    in_t = pltpu.make_async_copy(tok_in, tok, out_sems.at[2])
+    in_t.start()
+    barrier = pltpu.get_barrier_semaphore()
+    partners = to_plane + to_seq
+    for dev in partners:
+        pl.semaphore_signal(barrier, inc=1, device_id=dev, device_id_type=MESH)
 
     w0[s, z, x, :, 0:sw] = wqkv_in[1]
     w0[s, z, x, :, sw : 2 * sw] = wqkv_in[2]
     w0[s, z, x, :, 2 * sw : 3 * sw] = wqkv_in[0]
     w0[s, z, x, :, 3 * sw : 4 * sw] = wo_in[...]
     w1[s, z, x] = win_in[...]
-    w2[s, z, x] = turn(wdn_in[...])
+    w2[s, z, x] = wdn_in[...]
     place = (
         lax.broadcasted_iota(jnp.int32, (bd, 2 * bd), 1)
         == lax.broadcasted_iota(jnp.int32, (bd, 2 * bd), 0) + bd * x
@@ -583,39 +636,228 @@
     nb[s, z, x] = nn(
         jnp.broadcast_to(nrm_in[...], (PAD, bd)), jnp.where(place, 1.0, 0.0).astype(LOW)
     ).astype(LOW)
-
-    barrier = pltpu.get_barrier_semaphore()
-    partners = [to_core, to_y, to_x] + to_z
-    for dev in partners:
-        pl.semaphore_signal(barrier, inc=1, device_id=dev, device_id_type=MESH)
     pl.semaphore_wait(barrier, len(partners))
 
-    def spread_z(ref):
-        return [wires.send(ref.at[s, z, x], ref.at[s, z, x], dev) for dev in to_z]
-
-    def spread_z_half(ref, lo, hi):
+    tasks, steps = {}, {}
+    plan = list(PLAN)
+
+    def go(name):
+        steps[name] += 1
+        next(tasks[name], None)
+
+    def poll():
+        for name in plan.pop(0) if plan else ():
+            go(name)
+
+    def need(name, step):
+        while steps[name] < step:
+            go(name)
+
+    def gather_norm():
+        at = nb.at[s, z, x]
+        first = [wires.send(at, at, dev) for dev in to_plane]
+        yield
+        arrived(first)
+        at = nb.at[s]
+        second = [wires.send(at, at, dev) for dev in to_seq]
+        yield
+        arrived(second)
+        yield
+
+    def gather_plane(ref, lo, hi):
         at = ref.at[s, z, x, :, lo:hi]
-        return [wires.send(at, at, dev) for dev in to_z]
-
-    n_z = spread_z(nb)
-    kv_z = spread_z_half(w0, 0, 2 * sw)
+        first = [wires.send(at, at, dev) for dev in to_plane]
+        yield
+        arrived(first)
+        at = ref.at[s, :, :, :, lo:hi]
+        near = [wires.send(at, at, to_core)]
+        far = [wires.send(at, at, to_y)]
+        yield
+        arrived(near)
+        yield
+        arrived(far)
+        at = ref.at[s_y, :, :, :, lo:hi]
+        last = [wires.send(at, at, to_core)]
+        yield
+        arrived(last)
+        yield
+
+    def gather_zxy(ref, lo, hi):
+        at = ref.at[s, z, x, :, lo:hi]
+        now = [wires.send(at, at, dev) for dev in to_z]
+        yield
+        arrived(now)
+        at = ref.at[s, :, x, :, lo:hi]
+        now = [wires.send(at, at, to_x)]
+        yield
+        arrived(now)
+        at = ref.at[s, :, :, :, lo:hi]
+        near = [wires.send(at, at, to_core)]
+        far = [wires.send(at, at, to_y)]
+        yield
+        arrived(near)
+        yield
+        arrived(far)
+        at = ref.at[s_y, :, :, :, lo:hi]
+        last = [wires.send(at, at, to_core)]
+        yield
+        arrived(last)
+        yield
+
+    def gather_zyx(ref, lo, hi):
+        at = ref.at[s, z, x, :, lo:hi]
+        now = [wires.send(at, at, dev) for dev in to_z]
+        yield
+        arrived(now)
+        at = ref.at[s, :, x, :, lo:hi]
+        now = [wires.send(at, at, to_y)]
+        yield
+        arrived(now)
+        now = []
+        for side in (s, s_y):
+            at = ref.at[side, :, x, :, lo:hi]
+            now.append(wires.send(at, at, to_x))
+        yield
+        arrived(now)
+        now = []
+        for side in (s, s_y):
+            at = ref.at[side, :, :, :, lo:hi]
+            now.append(wires.send(at, at, to_core))
+        yield
+        arrived(now)
+        yield
+
+    def reduce_seq(k):
+        r1, r2, f = ar_r1.at[k], ar_r2.at[k], ar_f.at[k]
+        now = [wires.send(ar_a.at[2 * v + 1 - c], r1.at[v], to_core) for v in range(2)]
+        yield
+        arrived(now)
+        wires.left(now)
+        for v in range(2):
+            ar_a[2 * v + c] = ar_a[2 * v + c] + r1[v]
+        now = [wires.send(ar_a.at[2 * v + c], r2.at[v], to_y) for v in range(2)]
+        yield
+        arrived(now)
+        wires.left(now)
+        for v in range(2):
+            f[2 * v + c] = ar_a[2 * v + c] + r2[v]
+        now = [wires.send(f.at[2 * v + c], f.at[2 * v + c], to_core) for v in range(2)]
+        yield
+        arrived(now)
+        yield
+
+    def scatter_start(g, lo, hi, rc):
+        now = [
+            wires.send(g.at[2 * v + 1 - c, :, :, :, lo:hi], rc.at[v], to_core) for v in range(2)
+        ]
+        yield
+        arrived(now)
+        for v in range(2):
+
+            def add(j, carry):
+                at = (2 * v + c, j, slice(None), slice(None), slice(lo, hi))
+                g[at] = g[at] + rc[v, j]
+                return carry
+
+            lax.fori_loop(0, nz, add, 0)
+
+    def scatter_end(g, lo, hi, rz):
+        now = [
+            wires.send(g.at[s, lax.rem(z + k, nz), x, :, lo:hi], rz.at[k - 1], to_z[k - 1])
+            for k in range(1, nz)
+        ]
+        yield
+        arrived(now)
+        yield
+
+    def scatter_yxz(g, lo, hi, rc, ra, rb, rz):
+        yield from scatter_start(g, lo, hi, rc)
+        now = [wires.send(g.at[2 * (1 - y) + c, :, :, :, lo:hi], ra, to_y)]
+        yield
+        arrived(now)
+
+        def add(j, carry):
+            g[s, j, :, :, lo:hi] = g[s, j, :, :, lo:hi] + ra[j]
+            return carry
+
+        lax.fori_loop(0, nz, add, 0)
+        now = [wires.send(g.at[s, :, 1 - x, :, lo:hi], rb, to_x)]
+        yield
+        arrived(now)
+        g[s, :, x, :, lo:hi] = g[s, :, x, :, lo:hi] + rb[...]
+        yield from scatter_end(g, lo, hi, rz)
+
+    def scatter_xyz(g, lo, hi, rc, ra, rb, rz):
+        yield from scatter_start(g, lo, hi, rc)
+        now = [
+            wires.send(g.at[2 * v + c, :, 1 - x, :, lo:hi], rb.at[v], to_x) for v in range(2)
+        ]
+        yield
+        arrived(now)
+        for v in range(2):
+            g[2 * v + c, :, x, :, lo:hi] = g[2 * v + c, :, x, :, lo:hi] + rb[v]
+        now = [wires.send(g.at[2 * (1 - y) + c, :, x, :, lo:hi], ra, to_y)]
+        yield
+        arrived(now)
+        g[s, :, x, :, lo:hi] = g[s, :, x, :, lo:hi] + ra[...]
+        yield from scatter_end(g, lo, hi, rz)
+
+    def scattered(name):
+        g, lo, hi, rz = scattered_parts[name]
+        total = g[s, z, x, :, lo:hi].astype(WIDE)
+        for k in range(nz - 1):
+            total = total + rz[k].astype(WIDE)
+        return total
+
+    def add_task(name, task):
+        tasks[name], steps[name] = task, 0
+
+    half = w1.shape[4] // 2
+    gathers = {"plane": gather_plane, "zxy": gather_zxy, "zyx": gather_zyx}
+    add_task("norm", gather_norm())
+    add_task("kv", gathers[KIND["kv"]](w0, 0, 2 * sw))
+    add_task("qo", gathers[KIND["qo"]](w0, 2 * sw, 4 * sw))
+    for name, ref in (("w1", w1), ("w2", w2)):
+        add_task(name + "a", gathers[KIND[name + "a"]](ref, 0, half))
+        add_task(name + "b", gathers[KIND[name + "b"]](ref, half, 2 * half))
+    add_task("ar1", reduce_seq(0))
+    add_task("ar2", reduce_seq(1))
+    scattered_parts = {}
+    for n, (name, kind, g, lo, hi) in enumerate(
+        scatter_parts(g0, g1, g2, sw, half)
+    ):
+        rc, ra, rb, rz = scatter_refs[4 * n : 4 * n + 4]
+        make = scatter_yxz if kind == "yxz" else scatter_xyz
+        add_task(name, make(g, lo, hi, rc, ra, rb, rz))
+        scattered_parts[name] = (g, lo, hi, rz)
+
+    def own_ready(name, j):
+        need(name, OWN_STEP[KIND[name]][j])
+
+    poll()
 
     seq_pos = s * rows
     long_from = ls[0, 0]
     long_to = long_from + ns * rows - SHORT
+    blocks = [s, s_core, s_y, s_far]
 
     def shared_mask(position):
         at = position + seq_pos
         return jnp.where((at >= long_from) & (at < long_to), 1.0, 0.0)
 
+    def tiles(lo, hi, step):
+        def body(t, carry):
+            step(t)
+            return carry
+
+        lax.fori_loop(lo, hi, body, 0)
+
     pos_row = pos[...]
     posc[...] = jnp.broadcast_to(pos_row.astype(WIDE), (128, slots)).T
     sh_r = shared_mask(pos_row)
 
-    def select_tile(t, carry):
+    def select_tile(t):
         at = pl.multiple_of(t * tile, tile)
-        row_id = lax.broadcasted_iota(jnp.int32, (tile, slots), 0) + at
-        pt[pl.ds(at, tile), :] = jnp.where(row_id == pos_row, 1.0, 0.0).astype(LOW)
         for j in range(tile // 128):
             lane = lax.broadcasted_iota(jnp.int32, (slots, 128), 1) + (at + 128 * j)
             pm[:, pl.ds(at + 128 * j, 128)] = jnp.where(
@@ -627,30 +869,18 @@
         ones = jnp.where(row == 0, sh, jnp.where(row == 1, 1.0 - sh, 0.0)).astype(LOW)
         for h in range(heads):
             vs[h, 2 * size : 2 * size + PAD, pl.ds(at, tile)] = ones
-        return carry
-
-    lax.fori_loop(0, rows // tile, select_tile, 0)
+
+    tiles(0, rows // tile, select_tile)
+    poll()
     for h in range(heads):
         rft[h] = turn(rf[h])
-
-    arrived(n_z)
-    at = nb.at[s, :, x]
-    n_x = [wires.send(at, at, to_x)]
+    in_t.wait()
     toks_r = nn(pm[...], tok[...])
-    arrived(n_x)
-    at = nb.at[s]
-    n_y = [wires.send(at, at, to_y)]
+    poll()
+    need("norm", 2)
     unit_r, _ = unit_norm(toks_r)
-    arrived(n_y)
-    n_c = []
-    for side in (s, s_y):
-        at = nb.at[side]
-        n_c.append(wires.send(at, at, to_core))
-    arrived(kv_z)
-    at = w0.at[s, :, x, :, 0 : 2 * sw]
-    kv_x = [wires.send(at, at, to_x)]
-    qo_z = spread_z_half(w0, 2 * sw, 4 * sw)
-    arrived(n_c)
+    poll()
+    need("norm", 3)
 
     def norm_row(i):
         return jnp.concatenate(
@@ -665,40 +895,31 @@
     xn_r = (unit_r * gain1 + bias1).astype(LOW)
     xnrt[...] = turn(xn_r)
 
-    def norm_tile(t, carry):
+    def norm_tile(t):
         at = pl.multiple_of(t * tile, tile)
         unit, _ = unit_norm(tok[pl.ds(at, tile), :].astype(WIDE))
         xnt[:, pl.ds(at, tile)] = turn((unit * gain1 + bias1).astype(LOW))
-        return carry
-
-    lax.fori_loop(0, rows // tile, norm_tile, 0)
-
-    arrived(kv_x)
-    at = w0.at[s, :, :, :, 0 : 2 * sw]
-    kv_y = [wires.send(at, at, to_y)]
-    kv_c = [wires.send(at, at, to_core)]
-    w1_z = spread_z(w1)
-
-    def kv_block(sd):
-        wkvt[sd] = turn(flat(w0[sd, :, :, :, 0 : 2 * sw]))
-
-        def step(t, carry):
-            at = pl.multiple_of(t * wide_tile, wide_tile)
-            cols = pl.ds(at, wide_tile)
-            r = nn(wkvt[sd], xnt[:, cols]).astype(LOW)
-            kvt[sd, :, cols] = r
-            lane = lax.broadcasted_iota(jnp.int32, (1, wide_tile), 1) + at
-            sh = shared_mask(lane).astype(LOW)
-            for i in range(2):
-                h = 2 * sd + i
-                k_h = r[size * i : size * (i + 1)]
-                v_h = r[sw + size * i : sw + size * (i + 1)]
-                kft[h, :, cols] = features(nn(rft[h], k_h), k_h, scale, feat).astype(LOW)
-                vs[h, 0:size, cols] = v_h * sh
-                vs[h, size : 2 * size, cols] = v_h * (1.0 - sh)
-            return carry
-
-        lax.fori_loop(0, rows // wide_tile, step, 0)
+
+    for n in range(3):
+        tiles(2 * n, 2 * n + 2, norm_tile)
+        poll()
+
+    def kv_tile(sd, t):
+        at = pl.multiple_of(t * wide_tile, wide_tile)
+        cols = pl.ds(at, wide_tile)
+        r = nn(wkvt[sd], xnt[:, cols]).astype(LOW)
+        kvt[sd, :, cols] = r
+        lane = lax.broadcasted_iota(jnp.int32, (1, wide_tile), 1) + at
+        sh = shared_mask(lane).astype(LOW)
+        for i in range(2):
+            h = 2 * sd + i
+            k_h = r[size * i : size * (i + 1)]
+            v_h = r[sw + size * i : sw + size * (i + 1)]
+            kft[h, :, cols] = features(nn(rft[h], k_h), k_h, scale, feat).astype(LOW)
+            vs[h, 0:size, cols] = v_h * sh
+            vs[h, size : 2 * size, cols] = v_h * (1.0 - sh)
+
+    def kv_sums(sd):
         for i in range(2):
             h = 2 * sd + i
             part = nt(vs[h], kft[h]).astype(LOW)
@@ -706,93 +927,50 @@
             ar_a[sd, i, size : size + PAD, :] = part[2 * size :]
             loc[h] = part[size:]
 
-    arrived(kv_c)
-
-    def kv_first(j, carry):
-        kv_block(s + j * (s_core - s))
-        return carry
-
-    lax.fori_loop(0, 2, kv_first, 0)
-
-    arrived(qo_z)
-    at = w0.at[s, :, x, :, 2 * sw : 4 * sw]
-    qo_x = [wires.send(at, at, to_x)]
-    arrived(kv_y)
-    at = w0.at[s_y, :, :, :, 0 : 2 * sw]
-    kv_c2 = [wires.send(at, at, to_core)]
-    arrived(w1_z)
-    w2_z = spread_z(w2)
-    at = w1.at[s, :, x]
-    w1_x = [wires.send(at, at, to_x)]
-    arrived(kv_c2)
-
-    def kv_second(j, carry):
-        base = s_y
-        kv_block(base + j * (s_core - s))
-        return carry
-
-    lax.fori_loop(0, 2, kv_second, 0)
-
-    def reduce_first(buf, r1):
-        return [
-            wires.send(buf.at[2 * yy + 1 - c], r1.at[yy], to_core) for yy in range(2)
-        ]
-
-    def reduce_second(buf, r1, r2, f, copies):
-        arrived(copies)
-        wires.left(copies)
-        for yy in range(2):
-            mine = 2 * yy + c
-            buf[mine] = (buf[mine].astype(WIDE) + r1[yy].astype(WIDE)).astype(LOW)
-        return [wires.send(buf.at[2 * yy + c], r2.at[yy], to_y) for yy in range(2)]
-
-    def reduce_third(buf, r1, r2, f, copies):
-        arrived(copies)
-        wires.left(copies)
-        for yy in range(2):
-            mine = 2 * yy + c
-            f[mine] = (buf[mine].astype(WIDE) + r2[yy].astype(WIDE)).astype(LOW)
-        return [wires.send(f.at[2 * yy + c], f.at[2 * yy + c], to_core) for yy in range(2)]
-
-    ar1 = reduce_first(ar_a, ar_r1.at[0])
-    arrived(qo_x)
-    at = w0.at[s, :, :, :, 2 * sw : 4 * sw]
-    qo_c = [wires.send(at, at, to_core)]
-    qo_y = [wires.send(at, at, to_y)]
-    ar1 = reduce_second(ar_a, ar_r1.at[0], ar_r2.at[0], ar_f.at[0], ar1)
-    arrived(w1_x)
-    at = w1.at[s]
-    w1_y = [wires.send(at, at, to_y)]
-    w1_c = [wires.send(at, at, to_core)]
-    arrived(w2_z)
-    at = w2.at[s, :, x]
-    w2_x = [wires.send(at, at, to_x)]
-    arrived(qo_y)
-    at = w0.at[s_y, :, :, :, 2 * sw : 4 * sw]
-    qo_c2 = [wires.send(at, at, to_core)]
-    ar1 = reduce_third(ar_a, ar_r1.at[0], ar_r2.at[0], ar_f.at[0], ar1)
-    arrived(qo_c)
-    arrived(qo_c2)
-    for i in range(ns):
-        wqt[sw * i : sw * (i + 1), :] = turn(flat(w0[i, :, :, :, 2 * sw : 3 * sw]))
-        wo[:, sw * i : sw * (i + 1)] = flat(w0[i, :, :, :, 3 * sw : 4 * sw])
-
-    qr = nn(wqt[...], xnrt[...]).astype(LOW)
-    for h in range(heads):
-        q_h = qr[size * h : size * (h + 1)]
-        qrt[h] = q_h
-        qfr[h] = features(nn(rft[h], q_h), q_h, scale, feat).astype(LOW)
-
-    arrived(ar1)
+    for j, sd in enumerate(blocks):
+        own_ready("kv", j)
+        wkvt[sd] = turn(flat(w0[sd, :, :, :, 0 : 2 * sw]))
+        tiles(0, rows // wide_tile, functools.partial(kv_tile, sd))
+        poll()
+        kv_sums(sd)
+        poll()
+    poll()
+
+    keep = (g0, g1, g2)
+
+    def q_block(sd):
+        wqt[sd] = turn(flat(w0[sd, :, :, :, 2 * sw : 3 * sw]))
+        for t, gt in enumerate(keep):
+            cols = slice(t * wide_tile, (t + 1) * wide_tile)
+            q = nn(wqt[sd], xnt[:, cols]).astype(LOW)
+            for i in range(2):
+                q_h = q[size * i : size * (i + 1)]
+                qf = features(nn(rft[2 * sd + i], q_h), q_h, scale, feat).astype(LOW)
+                gt[sd, 2 * i : 2 * i + 2] = qf.reshape((2,) + g0.shape[2:4] + (wide_tile,))
+        q = nn(wqt[sd], xnrt[...]).astype(LOW)
+        for i in range(2):
+            q_h = q[size * i : size * (i + 1)]
+            qrt[2 * sd + i] = q_h
+            qfr[2 * sd + i] = features(nn(rft[2 * sd + i], q_h), q_h, scale, feat).astype(LOW)
+
+    for j, sd in enumerate(blocks):
+        own_ready("qo", j)
+        q_block(sd)
+        poll()
+    need("ar1", 4)
+
+    def tail_rows(k, h):
+        first = lax.broadcasted_iota(jnp.int32, (PAD, feat), 0) == 0
+        return jnp.where(
+            first,
+            ar_f[k, h // 2, h % 2, size : size + PAD, :].astype(WIDE),
+            loc[h, size : size + PAD, :].astype(WIDE),
+        ).astype(LOW)
+
     for h in range(heads):
         sumf[h, 0:size, :] = ar_f[0, h // 2, h % 2, 0:size, :]
         sumf[h, size : 2 * size, :] = loc[h, 0:size, :]
-        first = lax.broadcasted_iota(jnp.int32, (PAD, feat), 0) == 0
-        sumf[h, 2 * size : 2 * size + PAD, :] = jnp.where(
-            first,
-            ar_f[0, h // 2, h % 2, size : size + PAD, :].astype(WIDE),
-            loc[h, size : size + PAD, :].astype(WIDE),
-        ).astype(LOW)
+        sumf[h, 2 * size : 2 * size + PAD, :] = tail_rows(0, h)
 
     def split_ratio(nd, sh):
         pick = jnp.broadcast_to(sh, (size, sh.shape[1])) > 0.5
@@ -805,7 +983,25 @@
         num_r[h] = num
         den_r[h] = jnp.broadcast_to(den, (8, slots))
         hort[size * h : size * (h + 1), :] = (num * (1.0 / den)).astype(LOW)
-
+    poll()
+
+    for t, gt in enumerate(keep):
+        cols = slice(t * wide_tile, (t + 1) * wide_tile)
+        lane = lax.broadcasted_iota(jnp.int32, (1, wide_tile), 1) + t * wide_tile
+        sh = shared_mask(lane)
+
+        def attend(i, gt=gt, cols=cols, sh=sh):
+            for jj in range(2):
+                h = 2 * i + jj
+                qf = gt[i, 2 * jj : 2 * jj + 2].reshape(feat, wide_tile)
+                num, den = split_ratio(nn(sumf[h], qf), sh)
+                hot[h, :, cols] = (num * (1.0 / den)).astype(LOW)
+
+        tiles(0, ns, attend)
+        poll()
+
+    for i in range(ns):
+        wo[:, sw * i : sw * (i + 1)] = flat(w0[i, :, :, :, 3 * sw : 4 * sw])
     middle_r = toks_r + nn(turn(hort[...]), wo[...])
     unit2, inv2 = unit_norm(middle_r)
     xn2_r = (unit2 * gain2 + bias2).astype(LOW)
@@ -814,86 +1010,28 @@
     cot = mg[...].astype(WIDE) * jnp.where(slot_id < cnt[0, 0], 1.0, 0.0)
     cot_low = cot.astype(LOW)
     cot_t = turn(cot_low)
-
-    arrived(w2_x)
-    at = w2.at[s]
-    w2_y = [wires.send(at, at, to_y)]
-    w2_c = [wires.send(at, at, to_core)]
-    arrived(w1_y)
-    at = w1.at[s_y]
-    w1_c2 = [wires.send(at, at, to_core)]
-    arrived(w2_y)
-    at = w2.at[s_y]
-    w2_c2 = [wires.send(at, at, to_core)]
-    arrived(w1_c)
-    arrived(w2_c)
-    arrived(w1_c2)
-    arrived(w2_c2)
+    poll()
 
     dn2 = jnp.zeros((slots, width), WIDE)
-    for i in range(ns):
-        win = flat(w1[i])
+    for j, sd in enumerate(blocks):
+        for name in ("w1a", "w1b", "w2a", "w2b"):
+            own_ready(name, j)
+        win = flat(w1[sd])
         upper = nn(xn2_r, win)
         cdf = 0.5 + 0.5 * lax.erf(upper * ROOT_HALF)
         act = (upper * cdf).astype(LOW)
         slope = cdf + upper * (PDF_SCALE * jnp.exp(-0.5 * upper * upper))
-        du = (nn(cot_low, flat(w2[i])) * slope).astype(LOW)
-        g1[i] = nn(xn2_rt, du).astype(LOW).reshape(g1.shape[1:])
-        g2[i] = nn(cot_t, act).astype(LOW).reshape(g2.shape[1:])
+        du = (nn(cot_low, flat(w2[sd])) * slope).astype(LOW)
+        g2[sd] = nn(cot_t, act).astype(LOW).reshape(g2.shape[1:])
+        g1[sd] = nn(xn2_rt, du).astype(LOW).reshape(g1.shape[1:])
         dn2 = dn2 + nt(du, win)
-
-    def scatter_first(g, rc):
-        return [wires.send(g.at[2 * yy + 1 - c], rc.at[yy], to_core) for yy in range(2)]
-
-    def scatter_add_core(g, rc, copies):
-        arrived(copies)
-        for yy in range(2):
-            def step(j, carry):
-                g[2 * yy + c, j] = (g[2 * yy + c, j].astype(WIDE) + rc[yy, j].astype(WIDE)).astype(LOW)
-                return carry
-            lax.fori_loop(0, nz, step, 0)
-
-    def scatter_y(g, ra):
-        return [wires.send(g.at[2 * (1 - y) + c], ra, to_y)]
-
-    def scatter_y_add(g, ra, copies):
-        arrived(copies)
-        def step(j, carry):
-            g[s, j] = (g[s, j].astype(WIDE) + ra[j].astype(WIDE)).astype(LOW)
-            return carry
-        lax.fori_loop(0, nz, step, 0)
-
-    def scatter_x(g, rb):
-        return [wires.send(g.at[s, :, 1 - x], rb, to_x)]
-
-    def scatter_x_add(g, rb, copies):
-        arrived(copies)
-        g[s, :, x] = (g[s, :, x].astype(WIDE) + rb[...].astype(WIDE)).astype(LOW)
-
-    def scatter_z(g, rz):
-        return [
-            wires.send(g.at[s, lax.rem(z + k, nz), x], rz.at[k - 1], to_z[k - 1])
-            for k in range(1, nz)
-        ]
-
-    def scatter_done(g, rz, copies):
-        arrived(copies)
-        total = g[s, z, x].astype(WIDE)
-        for k in range(nz - 1):
-            total = total + rz[k].astype(WIDE)
-        return total
-
-    s1 = scatter_first(g1, rc1)
-    s2 = scatter_first(g2, rc2)
+        poll()
+    poll()
 
     norm_g2 = jnp.sum(dn2 * unit2, axis=0, keepdims=True)
     norm_g3 = jnp.sum(dn2, axis=0, keepdims=True)
-    dm = cot + norm_back(dn2, unit2, inv2, gain2)
-    d_att = dm.astype(LOW)
+    d_att = (cot + norm_back(dn2, unit2, inv2, gain2)).astype(LOW)
     dmid_low[...] = d_att
-    for i in range(ns):
-        part = nn(hort[...], d_att[:, sw * i : sw * (i + 1)]).astype(LOW)
-        gqo[i, :, :, :, sw : 2 * sw] = part.reshape(gqo.shape[1:4] + (sw,))
     dhd[...] = nt(wo[...], d_att)
     for h in range(heads):
         dh = dhd[size * h : size * (h + 1), :]
@@ -912,12 +1050,8 @@
         ar_a[h // 2, h % 2, 0:size, :] = part[0:size]
         ar_a[h // 2, h % 2, size : size + PAD, :] = part[2 * size :]
         loc[h] = part[size:]
-    ar2 = reduce_first(ar_a, ar_r1.at[1])
-    scatter_add_core(g1, rc1, s1)
-    s1 = scatter_y(g1, ra1)
-    scatter_add_core(g2, rc2, s2)
-    s2 = [wires.send(g2.at[2 * yy + c, :, 1 - x], rb2.at[yy], to_x) for yy in range(2)]
-    ar2 = reduce_second(ar_a, ar_r1.at[1], ar_r2.at[1], ar_f.at[1], ar2)
+    poll()
+    poll()
 
     for h in range(heads):
         d_qf = nn(turn(sumf[h]), dn_st[h])
@@ -927,28 +1061,24 @@
         dqt[size * h : size * (h + 1), :] = (
             scale * nn(rf[h], w.astype(LOW)) - (scale * scale) * q_h * ws
         ).astype(LOW)
+    poll()
     for i in range(ns):
         part = nt(xnrt[...], dqt[sw * i : sw * (i + 1), :]).astype(LOW)
-        gqo[i, :, :, :, 0:sw] = part.reshape(gqo.shape[1:4] + (sw,))
-    s0 = scatter_first(gqo, rc_qo)
+        g0[i, :, :, :, 2 * sw : 3 * sw] = part.reshape(g0.shape[1:4] + (sw,))
+        part = nn(hort[...], d_att[:, sw * i : sw * (i + 1)]).astype(LOW)
+        g0[i, :, :, :, 3 * sw : 4 * sw] = part.reshape(g0.shape[1:4] + (sw,))
     acc = jnp.zeros((width, slots), WIDE)
     for i in range(ns):
         acc = acc + nn(flat(w0[i, :, :, :, 2 * sw : 3 * sw]), dqt[sw * i : sw * (i + 1), :])
     dxqt[...] = acc.astype(LOW)
-    ar2 = reduce_third(ar_a, ar_r1.at[1], ar_r2.at[1], ar_f.at[1], ar2)
+    poll()
+    poll()
 
     def dense_tile(t):
         at = pl.multiple_of(t * tile, tile)
         cols = pl.ds(at, tile)
-        q = nn(wqt[...], xnt[:, cols]).astype(LOW)
-        lane = lax.broadcasted_iota(jnp.int32, (1, tile), 1) + at
-        sh = shared_mask(lane)
-        for h in range(heads):
-            q_h = q[size * h : size * (h + 1)]
-            qf = features(nn(rft[h], q_h), q_h, scale, feat).astype(LOW)
-            num, den = split_ratio(nn(sumf[h], qf), sh)
-            hot[size * h : size * (h + 1), :] = (num * (1.0 / den)).astype(LOW)
-        mid = tok[cols, :].astype(WIDE) + nn(turn(hot[...]), wo[...])
+        ho = turn(flat(hot[:, :, cols]))
+        mid = tok[cols, :].astype(WIDE) + nn(ho, wo[...])
         unit, _ = unit_norm(mid)
         xn2 = (unit * gain2 + bias2).astype(LOW)
         total = mid
@@ -958,73 +1088,47 @@
             total = total + nt(act, flat(w2[i]))
         mixed_v[cols, :] = total.astype(LOW)
 
-    def dense_loop(lo, hi):
-        def step(t, carry):
-            dense_tile(t)
-            return carry
-
-        lax.fori_loop(lo, hi, step, 0)
-
-    dense_loop(0, 2)
-
-    arrived(ar2)
+    for n in range(EARLY):
+        tiles(n, n + 1, dense_tile)
+        poll()
+    need("ar2", 4)
+
     for h in range(heads):
-        first = lax.broadcasted_iota(jnp.int32, (PAD, feat), 0) == 0
-        tail = jnp.where(
-            first,
-            ar_f[1, h // 2, h % 2, size : size + PAD, :].astype(WIDE),
-            loc[h, size : size + PAD, :].astype(WIDE),
-        ).astype(LOW)
-        stack = jnp.concatenate([ar_f[1, h // 2, h % 2, 0:size, :], loc[h, 0:size, :], tail], axis=0)
+        stack = jnp.concatenate(
+            [ar_f[1, h // 2, h % 2, 0:size, :], loc[h, 0:size, :], tail_rows(1, h)], axis=0
+        )
         ar_a[h // 2, h % 2, 0:size, :] = stack[0:size]
         dsumt[h] = turn(stack)
-
-    scatter_y_add(g1, ra1, s1)
-    s1 = scatter_x(g1, rb1)
-    arrived(s2)
-    for yy in range(2):
-        g2[2 * yy + c, :, x] = (g2[2 * yy + c, :, x].astype(WIDE) + rb2[yy].astype(WIDE)).astype(LOW)
-    s2 = [wires.send(g2.at[2 * (1 - y) + c, :, x], ra2, to_y)]
-
-    def key_block(sd, carry):
-        def step(t, carry2):
-            at = pl.multiple_of(t * wide_tile, wide_tile)
-            cols = pl.ds(at, wide_tile)
-            lane = lax.broadcasted_iota(jnp.int32, (1, wide_tile), 1) + at
-            sh = shared_mask(lane)
-            pick = jnp.broadcast_to(sh, (size, wide_tile)) > 0.5
-            for i in range(2):
-                h = 2 * sd + i
-                kf = kft[h, :, cols]
-                w = nn(dsumt[h], vs[h, :, cols]) * kf.astype(WIDE)
-                ws = jnp.sum(w, axis=0, keepdims=True)
-                k_h = kvt[sd, size * i : size * (i + 1), cols].astype(WIDE)
-                dk = scale * nn(rf[h], w.astype(LOW)) - (scale * scale) * k_h * ws
-                dva = nn(ar_a[sd, i, 0:size, :], kf)
-                dvb = nn(loc[h, 0:size, :], kf)
-                kvt[sd, size * i : size * (i + 1), cols] = dk.astype(LOW)
-                kvt[sd, sw + size * i : sw + size * (i + 1), cols] = jnp.where(pick, dva, dvb).astype(LOW)
-            return carry2
-
-        lax.fori_loop(0, rows // wide_tile, step, 0)
-        gkv[sd] = nt(xnt[...], kvt[sd]).astype(LOW).reshape(gkv.shape[1:])
-        return carry
-
-    lax.fori_loop(0, ns, key_block, 0)
-    s3 = scatter_first(gkv, rc_kv)
-    scatter_add_core(gqo, rc_qo, s0)
-    s0 = scatter_y(gqo, ra_qo)
-    scatter_x_add(g1, rb1, s1)
-    s1 = scatter_z(g1, rz1)
-    arrived(s2)
-    g2[s, :, x] = (g2[s, :, x].astype(WIDE) + ra2[...].astype(WIDE)).astype(LOW)
-    s2 = scatter_z(g2, rz2)
-    scatter_add_core(gkv, rc_kv, s3)
-    s3 = scatter_y(gkv, ra_kv)
+    poll()
+
+    def key_tile(sd, t):
+        at = pl.multiple_of(t * wide_tile, wide_tile)
+        cols = pl.ds(at, wide_tile)
+        lane = lax.broadcasted_iota(jnp.int32, (1, wide_tile), 1) + at
+        sh = shared_mask(lane)
+        pick = jnp.broadcast_to(sh, (size, wide_tile)) > 0.5
+        for i in range(2):
+            h = 2 * sd + i
+            kf = kft[h, :, cols]
+            w = nn(dsumt[h], vs[h, :, cols]) * kf.astype(WIDE)
+            ws = jnp.sum(w, axis=0, keepdims=True)
+            k_h = kvt[sd, size * i : size * (i + 1), cols].astype(WIDE)
+            dk = scale * nn(rf[h], w.astype(LOW)) - (scale * scale) * k_h * ws
+            dva = nn(ar_a[sd, i, 0:size, :], kf)
+            dvb = nn(loc[h, 0:size, :], kf)
+            kvt[sd, size * i : size * (i + 1), cols] = dk.astype(LOW)
+            kvt[sd, sw + size * i : sw + size * (i + 1), cols] = jnp.where(pick, dva, dvb).astype(LOW)
+
+    for sd in (s_core, s_far, s_y, s):
+        tiles(0, rows // wide_tile, functools.partial(key_tile, sd))
+        poll()
+        part = nt(xnt[...], kvt[sd]).astype(LOW)
+        g0[sd, :, :, :, 0 : 2 * sw] = part.reshape(g0.shape[1:4] + (2 * sw,))
+        poll()
 
     ng_a[...] = jnp.zeros(ng_a.shape, WIDE)
 
-    def token_tile(t, carry):
+    def token_tile(t):
         at = pl.multiple_of(t * tile, tile)
         cols = pl.ds(at, tile)
         dxt = nn(dxqt[...], pm[:, cols])
@@ -1032,62 +1136,74 @@
             dxt = dxt + nn(flat(w0[i, :, :, :, 0 : 2 * sw]), kvt[i, :, cols])
         dx = dxt.T
         unit, inv = unit_norm(tok[cols, :].astype(WIDE))
-        tgrad_v[cols, :] = norm_back(dx, unit, inv, gain1) + nn(pt[cols, :], dmid_low[...])
+        tgrad_v[cols, :] = norm_back(dx, unit, inv, gain1) + nn(turn(pm[:, cols]), dmid_low[...])
         ng_a[0:1, :] += jnp.sum(dx * unit, axis=0, keepdims=True)
         ng_a[1:2, :] += jnp.sum(dx, axis=0, keepdims=True)
-        return carry
-
-    lax.fori_loop(0, rows // tile, token_tile, 0)
+
+    for n in range(3):
+        tiles(2 * n, 2 * n + 2, token_tile)
+        poll()
     out_t = pltpu.make_async_copy(tgrad_v, tgrad_out, out_sems.at[0])
     out_t.start()
     ng_a[2:3, :] = norm_g2
     ng_a[3:4, :] = norm_g3
 
-    n_g = [wires.send(ng_a, ng_r.at[0], to_core)]
-    scatter_y_add(gqo, ra_qo, s0)
-    s0 = scatter_x(gqo, rb_qo)
-    scatter_y_add(gkv, ra_kv, s3)
-    s3 = scatter_x(gkv, rb_kv)
-    arrived(n_g)
-    wires.left(n_g)
-    ng_a[...] += ng_r[0]
-    n_g = [wires.send(ng_a, ng_r.at[1], to_y)]
-    dense_loop(2, 4)
-    arrived(n_g)
-    wires.left(n_g)
-    ng_a[...] += ng_r[1]
-    n_g = [wires.send(ng_a, ng_r.at[2], to_x)]
-    scatter_x_add(gqo, rb_qo, s0)
-    s0 = scatter_z(gqo, rz_qo)
-    scatter_x_add(gkv, rb_kv, s3)
-    s3 = scatter_z(gkv, rz_kv)
-    arrived(n_g)
-    wires.left(n_g)
-    ng_a[...] += ng_r[2]
-    n_g = [wires.send(ng_a, ng_r.at[2 + k], to_z[k - 1]) for k in range(1, nz)]
-    dense_loop(4, rows // tile)
+    def sum_norm():
+        order = [([to_core], 0), ([to_y], 1), ([to_x], 2), (to_z, 3)]
+        for devs, k in order:
+            now = [wires.send(ng_a, ng_r.at[k + n], dev) for n, dev in enumerate(devs)]
+            yield
+            arrived(now)
+            wires.left(now)
+            for n in range(len(devs)):
+                ng_a[...] += ng_r[k + n]
+        yield
+
+    add_task("ngs", sum_norm())
+    poll()
+    for n in range(EARLY, rows // tile):
+        tiles(n, n + 1, dense_tile)
+        poll()
     out_m = pltpu.make_async_copy(mixed_v, mixed_out, out_sems.at[1])
     out_m.start()
 
-    gin[...] = scatter_done(g1, rz1, s1)
-    gdn[...] = scatter_done(g2, rz2, s2).T
-    qo = scatter_done(gqo, rz_qo, s0)
-    kv = scatter_done(gkv, rz_kv, s3)
+    need("qog", 5)
+    for name in ("g2a", "g2b", "g1a", "g1b"):
+        need(name, 5)
+    gin[:, 0:half] = scattered("g1a")
+    gin[:, half:] = scattered("g1b")
+    gdn[:, 0:half] = scattered("g2a")
+    gdn[:, half:] = scattered("g2b")
+    qo = scattered("qog")
     gqkv[0] = qo[:, 0:sw]
-    gqkv[1] = kv[:, 0:sw]
-    gqkv[2] = kv[:, sw : 2 * sw]
     gop[...] = qo[:, sw : 2 * sw]
-    arrived(n_g)
+    for step in range(1, 6):
+        need("kg", step)
+        need("vg", step)
+        need("ngs", step)
+    gqkv[1] = scattered("kg")
+    gqkv[2] = scattered("vg")
     total = ng_a[...]
-    for k in range(1, nz):
-        total = total + ng_r[2 + k]
     row = lax.broadcasted_iota(jnp.int32, total.shape, 0)
     mine = jnp.sum(jnp.where(row == s, total, 0.0), axis=0, keepdims=True)
     mine = jnp.broadcast_to(mine, total.shape)
     gnorm[...] = pltpu.roll(mine, lax.rem(width - bd * b, width), 1)[0:1, 0:bd]
+    assert not plan
     wires.drain()
     out_t.wait()
     out_m.wait()
+
+
+def scatter_parts(g0, g1, g2, sw, half):
+    return (
+        ("g1a", "yxz", g1, 0, half),
+        ("g1b", "xyz", g1, half, 2 * half),
+        ("g2a", "yxz", g2, 0, half),
+        ("g2b", "xyz", g2, half, 2 * half),
+        ("qog", "xyz", g0, 2 * sw, 4 * sw),
+        ("kg", "yxz", g0, 0, sw),
+        ("vg", "xyz", g0, sw, 2 * sw),
+    )
 
 
 def fits(mesh, args):
@@ -1104,7 +1220,7 @@
         and sw == 2 * size
         and in_weight.shape[1] == 4 * sw
         and heads == 2 * ns
-        and rows % 512 == 0
+        and rows == 3 * 512
         and feat == 256
     )
 
@@ -1138,19 +1254,19 @@
     anywhere = pl.BlockSpec(memory_space=pl.ANY)
     tall = (nz, 2, bd)
     scratch = [
+        low(rows, width),
         low(ns, *tall, 4 * sw),
         low(ns, *tall, fw),
         low(ns, *tall, fw),
         low(ns, nz, 2, PAD, 2 * bd),
         low(ns, 2 * sw, width),
-        low(width, width),
+        low(ns, sw, width),
         low(width, width),
         low(width, rows),
         low(ns, 2 * sw, rows),
         low(heads, stack, rows),
         low(heads, feat, rows),
         low(slots, rows),
-        low(rows, slots),
         wide(slots, 128),
         low(heads, feat, size),
         low(heads, stack, feat),
@@ -1165,41 +1281,32 @@
         wide(heads, size, slots),
         wide(heads, 8, slots),
         low(heads, stack, slots),
-        low(width, 256),
+        low(heads, size, rows),
         low(width, slots),
         low(slots, width),
         low(width, slots),
         low(width, slots),
         wide(width, slots),
         low(width, slots),
-        low(ns, *tall, 2 * sw),
-        low(ns, *tall, 2 * sw),
+        low(ns, *tall, 4 * sw),
         low(ns, *tall, fw),
         low(ns, *tall, fw),
-        low(2, *tall, 2 * sw),
-        low(2, *tall, 2 * sw),
-        low(2, *tall, fw),
-        low(2, *tall, fw),
-        low(*tall, 2 * sw),
-        low(*tall, 2 * sw),
-        low(*tall, fw),
-        low(nz, bd, fw),
-        low(nz, bd, 2 * sw),
-        low(nz, bd, 2 * sw),
-        low(nz, bd, fw),
-        low(2, nz, bd, fw),
-        low(nz - 1, bd, 2 * sw),
-        low(nz - 1, bd, 2 * sw),
-        low(nz - 1, bd, fw),
-        low(nz - 1, bd, fw),
         wide(8, width),
         wide(2 + nz, 8, width),
         low(rows, width),
         wide(rows, width),
-        pltpu.SemaphoreType.DMA((96,)),
-        pltpu.SemaphoreType.DMA((96,)),
-        pltpu.SemaphoreType.DMA((2,)),
+        pltpu.SemaphoreType.DMA((160,)),
+        pltpu.SemaphoreType.DMA((160,)),
+        pltpu.SemaphoreType.DMA((3,)),
     ]
+    for _, kind, _, lo, hi in scatter_parts(None, None, None, sw, fw // 2):
+        n = hi - lo
+        scratch.append(low(2, *tall, n))
+        if kind == "yxz":
+            scratch += [low(*tall, n), low(nz, bd, n)]
+        else:
+            scratch += [low(nz, bd, n), low(2, nz, bd, n)]
+        scratch.append(low(nz - 1, bd, n))
     f32 = lambda *shape: jax.ShapeDtypeStruct(shape, WIDE)
     outs = pl.pallas_call(
         functools.partial(layer_kernel, nz, ns),
@@ -1209,10 +1316,10 @@
             f32(3, bd, sw),
             f32(bd, sw),
             f32(bd, fw),
-            f32(fw, bd),
+            f32(bd, fw),
             f32(1, bd),
         ),
-        in_specs=[vmem] * 7 + [smem, vmem, smem, vmem],
+        in_specs=[anywhere] + [vmem] * 6 + [smem, vmem, smem, vmem],
         out_specs=(anywhere, anywhere, vmem, vmem, vmem, vmem, vmem),
         scratch_shapes=scratch,
         compiler_params=pltpu.CompilerParams(
@@ -1224,7 +1331,7 @@
         qkv_weight,
         out_proj,
         in_weight,
-        out_weight,
+        out_weight.T,
         norm_params,
         rand_features,
         long_start.reshape(1, 1),
@@ -1232,7 +1339,7 @@
         masked_count,
         masked_grad.reshape(slots, width),
     )
-    return (outs[0][None], outs[1][None]) + outs[2:]
+    return (outs[0][None], outs[1][None]) + outs[2:5] + (outs[5].T, outs[6])
 
 
 def solution(mesh):

time: 162 us -> 118 us (0.73)
  Pallas kernels: 150 us -> 108 us
  local copies, waits for them, and re-layouts: 10.2 us -> 7.57 us
    pallas_call x1, Pallas kernels: 150 us -> 108 us  [fused_layer(): pl.pallas_call(functools.partial(layer_kernel, nz, ns), out_shape=(jax.Sh...]
    unnamed x18 -> x19, local copies, waits for them, and re-layouts: 10.2 us -> 7.57 us
where the time goes in v2:
time: 118 us; the launch traced here: 117 us
  Pallas kernels  108 us (92%)
  local copies, waits for them, and re-layouts  7.57 us (6%)
  between operations  1.97 us (2%)
    pallas_call x1, Pallas kernels, fused_layer(): pl.pallas_call(functools.partial(layer_kernel, nz, ns), out_shape=(jax.Sh...  108 us
    unnamed x19, local copies, waits for them, and re-layouts  7.57 us

profile of v2, /device:TPU:0, one launch (start us, length us, event | category | flops | bytes accessed | tf_op | source)
XLA Modules:
  0.0 117.4 jit_solution(17060355905558371930)
XLA Ops:
  1.9 107.9 %layer.1 = (bf16[1536,512]{1,0:T(8,128)(2,1)}, f32[1536,512]{1,0:T(8,128)}, f32[3,64,128]{2,1,0:T(8,128)}, f32[64,128]{1,0:T(8,128)}, f32[64,512]{1,0:T(8,128)}, /*index=5*/f32[64,512]{1,0:T(8,128)}, f32[1,64]{1,0:T(1,128)}) custom-call(bf16[1536,512]{1,0:T(8,128)(2,1)} %bitcast.9, bf16[3,64,128]{2,1,0:T(8,128)(2,1)} %wqkv_in.1, bf16[64,128]{1,0:T(8,128)(2,1)} %wo_in.1, ...), custom_call_target="tpu_custom_call" | custom-call | tf_op jit(solution)/shard_map/layer/pallas_call | solution.py:1311
  109.8 0.0 copy-start
  109.8 2.8 %copy.27 = bf16[1,1536,512]{2,1,0:T(8,128)(2,1)} copy(bf16[1,1536,512]{2,1,0:T(8,128)(2,1)} %bitcast.10) | data formatting | bytes 3145728
  112.6 0.0 copy-done
  112.6 0.0 copy-start.3
  112.6 0.0 copy-start.4
  112.6 0.0 copy-start.2
  112.6 0.0 copy-start.1
  112.6 0.0 copy-start.5
  112.7 1.7 %copy.28 = f32[1,1536,512]{2,1,0:T(8,128)} copy(f32[1,1536,512]{2,1,0:T(8,128)S(1)} %bitcast.8) | data formatting | bytes 6291456
  114.3 0.0 copy-done.3
  114.3 0.6 copy.29
  115.0 0.0 copy-done.4
  115.0 0.6 copy.30
  115.6 0.0 copy-done.2
  115.6 0.7 copy.31
  116.2 0.0 copy-done.1
  116.2 0.7 copy.32
  116.9 0.0 copy-done.5
  116.9 0.5 copy.33
Async XLA Ops:
  109.8 2.8 %copy-start = (f32[1536,512]{1,0:T(8,128)S(1)}, f32[1536,512]{1,0:T(8,128)}, u32[]{:S(2)}) copy-start(f32[1536,512]{1,0:T(8,128)} %get-tuple-element.15) | copy-start | bytes 9437188
  112.6 1.7 %copy-start.3 = (f32[3,64,128]{2,1,0:T(8,128)S(1)}, f32[3,64,128]{2,1,0:T(8,128)}, u32[]{:S(2)}) copy-start(f32[3,64,128]{2,1,0:T(8,128)} %get-tuple-element.30) | copy-start | bytes 294916
  112.6 2.3 %copy-start.4 = (f32[64,128]{1,0:T(8,128)S(1)}, f32[64,128]{1,0:T(8,128)}, u32[]{:S(2)}) copy-start(f32[64,128]{1,0:T(8,128)} %get-tuple-element.31) | copy-start | bytes 98308
  112.6 3.0 %copy-start.2 = (f32[64,512]{1,0:T(8,128)S(1)}, f32[64,512]{1,0:T(8,128)}, u32[]{:S(2)}) copy-start(f32[64,512]{1,0:T(8,128)} %get-tuple-element.32) | copy-start | bytes 393220
  112.6 3.6 %copy-start.1 = (f32[64,512]{1,0:T(8,128)S(1)}, f32[64,512]{1,0:T(8,128)}, u32[]{:S(2)}) copy-start(f32[64,512]{1,0:T(8,128)} %get-tuple-element.19) | copy-start | bytes 393220
  112.6 4.3 %copy-start.5 = (f32[1,64]{1,0:T(1,128)S(1)}, f32[1,64]{1,0:T(1,128)}, u32[]{:S(2)}) copy-start(f32[1,64]{1,0:T(1,128)} %get-tuple-element.34) | copy-start | bytes 772
